TPU v7x, 256 devices: a whole 4x4x8 slice. The times are simulated.
256 devices in a mesh: rows: 128 (over z, x, y), sub: 2 (over core).
Axes of the slice: x: 4, y: 4, z: 8, core: 2. Of those that a mesh axis runs over, the one named last changes fastest.
Arguments:
- locations: float32 [3, 524288], P(None, ('rows', 'sub')), may hold values from 0 to 1
- amplitude: float32 [524288], P(('rows', 'sub')), may hold values from 0.6 to 3.2
- noise: float32 [524288], P(('rows', 'sub')), may hold values from 0.25 to 1
- covariates: float32 [524288, 256], P(('rows', 'sub')), may hold values from -0.6 to 0.6
- pivot_owner: int32 [4, 128], replicated, may hold values from 0 to 255, as said below
- pivot_offset: int32 [4, 128], replicated, may hold values from 0 to 2047, as said below
Outputs:
- factor: float32 [524288, 512], P(('rows', 'sub'))
- weights: float32 [524288], P(('rows', 'sub'))
- mean_residual: float32 [4], replicated
Inputs may be any that keep to these rules, and one draw needn't show every extreme that they name: `pivot_owner`: an index of a device along rows+sub; in each block no device holds more than 2 pivots and some device holds exactly 2. `pivot_offset`: a row of the owner's shard; no (owner, offset) pair appears twice in the whole table.
All inputs are finite; a program needn't handle non-finite values.
Results may differ from a plain program's by a relative error of at most 0.0003.
Values sent between devices are 32-bit elements; how exact they have to be, the bound alone decides.
No kernel may reach another device: no remote copies, remote signals or barrier semaphores. Data moves between devices by JAX's collectives and lax.ppermute only.
A program may use at most 64 MiB of HBM per device.

v0:
```python
import jax
import jax.numpy as jnp
from jax import lax
from jax.experimental import pallas as pl
from jax.experimental.pallas import tpu as pltpu
from jax.sharding import Mesh
from jax.sharding import PartitionSpec as P

LENGTH_SCALE = 0.3
CAP = 2
AXES = ("z", "x", "y", "c")
HIGHEST = lax.Precision.HIGHEST
BLOCK = 128
PANEL = 16
SUB = 8
TILE = 256


def dot(left, right, dims):
    return lax.dot_general(
        left, right, (dims, ((), ())), precision=HIGHEST, preferred_element_type=jnp.float32
    )


def panel_inverse(low, high):
    sub = lax.broadcasted_iota(jnp.int32, (SUB, BLOCK), 0)
    low, high = list(low), list(high)
    root_low = jnp.zeros((SUB, BLOCK), jnp.float32)
    root_high = root_low
    for k in range(PANEL):
        if k < SUB:
            pivot = jnp.broadcast_to(low[k][k : k + 1, :], (SUB, BLOCK))
            inverse = pl.reciprocal(pivot, approx=True)
            take_low = jnp.where(sub > k, low[k] * inverse, 0.0)
            take_high = high[k] * inverse
            root_low = jnp.where(sub == k, lax.rsqrt(pivot), root_low)
            for j in range(PANEL):
                if j != k:
                    entry = low[j][k : k + 1, :]
                    low[j] = low[j] - take_low * entry
                    high[j] = high[j] - take_high * entry
            low[k] = jnp.where(sub == k, 1.0, -take_low)
            high[k] = -take_high
        else:
            s = k - SUB
            pivot = jnp.broadcast_to(high[k][s : s + 1, :], (SUB, BLOCK))
            inverse = pl.reciprocal(pivot, approx=True)
            take_high = jnp.where(sub > s, high[k] * inverse, 0.0)
            root_high = jnp.where(sub == s, lax.rsqrt(pivot), root_high)
            for j in range(PANEL):
                if j != k:
                    high[j] = high[j] - take_high * high[j][s : s + 1, :]
            high[k] = jnp.where(sub == s, 1.0, -take_high)
    return [low[j] * root_low for j in range(SUB)], [high[j] * root_high for j in range(PANEL)]


def block_inverse(rows):
    lane = lax.broadcasted_iota(jnp.int32, (SUB, BLOCK), 1)
    sub = lax.broadcasted_iota(jnp.int32, (SUB, BLOCK), 0)
    rows = list(rows)
    out = [None] * len(rows)
    for panel in range(BLOCK // PANEL):
        first = PANEL * panel
        at = 2 * panel

        def splat(piece, j):
            return jnp.broadcast_to(piece[:, first + j : first + j + 1], (SUB, BLOCK))

        rest = range(at + 2, len(rows))
        low = [splat(rows[at], j) for j in range(PANEL)]
        high = [splat(rows[at + 1], j) for j in range(PANEL)]
        coef = {r: [splat(rows[r], j) for j in range(PANEL)] for r in rest}
        inv_low, inv_high = panel_inverse(low, high)
        in_panel = (lane >= first) & (lane < first + PANEL)
        top = jnp.where(in_panel, jnp.where(lane - first == sub, 1.0, 0.0), rows[at])
        bottom = jnp.where(in_panel, jnp.where(lane - first - SUB == sub, 1.0, 0.0), rows[at + 1])
        new_low = jnp.zeros((SUB, BLOCK), jnp.float32)
        new_high = new_low
        for j in range(PANEL):
            entry = top[j : j + 1, :] if j < SUB else bottom[j - SUB : j - SUB + 1, :]
            if j < SUB:
                new_low = new_low + inv_low[j] * entry
            new_high = new_high + inv_high[j] * entry
        out[at] = jnp.where(lane <= first + sub, new_low, 0.0)
        out[at + 1] = jnp.where(lane <= first + SUB + sub, new_high, 0.0)
        if len(rest):
            weights = []
            for j in range(PANEL):
                term = inv_high[j] * new_high
                if j < SUB:
                    term = term + inv_low[j] * new_low
                weights.append(jnp.sum(term, axis=0, keepdims=True))
            for r in rest:
                piece = jnp.where(in_panel, 0.0, rows[r])
                for j in range(PANEL):
                    piece = piece - coef[r][j] * weights[j]
                rows[r] = piece
    return out


def factor_inverse(z_ref, r_ref):
    size = z_ref.shape[0]
    lane = lax.broadcasted_iota(jnp.int32, (1, size), 1)

    def step(b, carry):
        at = pl.ds(pl.multiple_of(b * BLOCK, BLOCK), BLOCK)
        pieces = [
            z_ref[pl.ds(pl.multiple_of(b * BLOCK + SUB * i, SUB), SUB), at]
            for i in range(BLOCK // SUB)
        ]
        inverse = jnp.concatenate(block_inverse(pieces), axis=0)
        r_ref[...] = dot(inverse, z_ref[at, :], ((1,), (0,)))
        r_ref[:, at] = inverse
        z_ref[:, at] = jnp.zeros((size, BLOCK), jnp.float32)
        row = r_ref[...]
        coef = jnp.where(lane >= (b + 1) * BLOCK, row, 0.0)
        z_ref[...] -= dot(coef, row, ((0,), (0,)))
        z_ref[at, :] = row
        return carry

    lax.fori_loop(0, size // BLOCK, step, 0)


def matern(cols, rows, col_scale, row_scale):
    dist_sq = None
    for axis_id in range(3):
        offset = cols[axis_id] - rows[axis_id]
        dist_sq = offset * offset if dist_sq is None else dist_sq + offset * offset
    scaled = dist_sq * lax.rsqrt(jnp.maximum(dist_sq, 1e-30))
    shape_term = (1.0 + scaled + dist_sq * (1.0 / 3.0)) * jnp.exp(-scaled)
    return col_scale * row_scale * shape_term


def main_kernel(
    mine_ref,
    other_ref,
    place_ref,
    match_ref,
    core_ref,
    feat_ref,
    cov_hbm,
    out_hbm,
    resid_ref,
    sums_ref,
    cov_ref,
    table_ref,
    scal_ref,
    z_ref,
    r_ref,
    col_ref,
    tile_ref,
    load_sem,
    store_sem,
):
    pivots = z_ref.shape[0]
    local_rows, cov_width = cov_ref.shape
    half = cov_width // 2
    planes = mine_ref.shape[0]
    blocks = pivots // BLOCK
    load = pltpu.make_async_copy(cov_hbm, cov_ref, load_sem)
    load.start()
    core = core_ref[0]

    per_block = BLOCK // blocks
    candidates = planes * per_block
    lane = lax.broadcasted_iota(jnp.int32, (SUB, BLOCK), 1)
    scale = (5.0**0.5) / LENGTH_SCALE
    for b in range(blocks):
        slots = pl.ds(b * per_block, per_block)
        pick = (
            lax.broadcasted_iota(jnp.int32, (BLOCK, candidates), 1) == place_ref[:, b : b + 1]
        ).astype(jnp.float32)
        own = dot(pick, mine_ref[:, slots, :].reshape(candidates, half), ((1,), (0,)))
        far = dot(pick, other_ref[:, slots, :].reshape(candidates, half), ((1,), (0,)))
        here = pl.ds(b * BLOCK, BLOCK)
        table_ref[here, :half] = jnp.where(core == 0, own, far)
        table_ref[here, half:] = jnp.where(core == 0, far, own)
        parts = []
        for q in range(planes // blocks):
            part = jnp.zeros((SUB, BLOCK), jnp.float32)
            for t in range(blocks):
                piece = mine_ref[q * blocks + t, BLOCK : BLOCK + SUB, :]
                shift = (per_block * (t - b)) % BLOCK
                piece = pltpu.roll(piece, shift, 1) if shift else piece
                part = jnp.where(lane // per_block == t, piece, part)
            parts.append(part)
        scalars = jnp.concatenate(parts, axis=1)
        scal_ref[:, here] = dot(scalars, pick, ((1,), (1,)))

    load.wait()
    for t in range(local_rows // BLOCK):
        at = pl.ds(t * BLOCK, BLOCK)
        col_ref[at, :] = feat_ref[:, at].T
    piv = scal_ref[...]
    piv_rows = [piv[i : i + 1, :] * scale for i in range(3)]
    piv_scale, piv_noise = piv[3:4, :], piv[4:5, :]

    for b in range(blocks):
        here = pl.ds(b * BLOCK, BLOCK)
        cols = scal_ref[:, here].T
        piece = matern([cols[:, i : i + 1] * scale for i in range(3)], piv_rows, cols[:, 3:4], piv_scale)
        same = lax.broadcasted_iota(jnp.int32, (BLOCK, 1), 0) + b * BLOCK == lax.broadcasted_iota(
            jnp.int32, (1, pivots), 1
        )
        piece = piece + jnp.where(same, piv_noise, 0.0)
        z_ref[here, :] = piece + dot(table_ref[here, :], table_ref[...], ((1,), (1,)))
    factor_inverse(z_ref, r_ref)

    match = match_ref[...]
    diagonal = lax.broadcasted_iota(jnp.int32, (BLOCK, BLOCK), 0) == lax.broadcasted_iota(
        jnp.int32, (BLOCK, BLOCK), 1
    )
    left = pivots // 2
    half_tiles = TILE // BLOCK

    def tile_step(t, taken):
        at = pl.ds(pl.multiple_of(t * TILE, TILE), TILE)
        cols = col_ref[at, :]
        cov = cov_ref[at, :]
        kernel = matern([cols[:, i : i + 1] * scale for i in range(3)], piv_rows, cols[:, 3:4], piv_scale)
        row_ids = lax.broadcasted_iota(jnp.int32, (TILE, 1), 0) + t * TILE
        kernel = kernel + jnp.where(row_ids == match, cols[:, 4:5], 0.0)
        kernel = kernel + dot(cov, table_ref[...], ((1,), (1,)))
        slot = lax.rem(t, 2)

        @pl.when(t >= 2)
        def _():
            pltpu.make_async_copy(tile_ref.at[slot], out_hbm.at[at, :], store_sem.at[slot]).wait()

        first = dot(kernel[:, :left], z_ref[:left, :left], ((1,), (1,)))
        second = dot(kernel, z_ref[left:, :], ((1,), (1,)))
        tile_ref[slot, :, :left] = first
        tile_ref[slot, :, left:] = second
        pltpu.make_async_copy(tile_ref.at[slot], out_hbm.at[at, :], store_sem.at[slot]).start()
        squares = []
        for b in range(blocks):
            source = first if b * BLOCK < left else second
            piece = source[:, (b * BLOCK) % left : (b * BLOCK) % left + BLOCK]
            squares.append(piece * piece)
        cov_sq = cov * cov
        total = cov_sq[:, :half] + cov_sq[:, half:]
        new_taken = []
        for b in range(blocks):
            total = total - squares[b]
            new_taken.append(
                taken[b] + jnp.sum(squares[b].reshape(TILE // SUB, SUB, BLOCK), axis=0)
            )
        cov_total = jnp.sum((cov_sq[:, :half] + cov_sq[:, half:]).reshape(TILE // SUB, SUB, BLOCK), axis=0)
        new_taken.append(taken[blocks] + cov_total)
        line = jnp.sum(total, axis=1, keepdims=True)
        for h in range(half_tiles):
            spread = jnp.where(diagonal, line[h * BLOCK : (h + 1) * BLOCK, :], 0.0)
            where = pl.ds(t * half_tiles + h, 1)
            resid_ref[where, :] = jnp.sum(spread, axis=0, keepdims=True)
        return tuple(new_taken)

    zero = jnp.zeros((SUB, BLOCK), jnp.float32)
    taken = lax.fori_loop(0, local_rows // TILE, tile_step, (zero,) * (blocks + 1))
    for slot in range(2):
        tile = local_rows // TILE - 2 + slot
        at = pl.ds(tile * TILE, TILE)
        pltpu.make_async_copy(tile_ref.at[tile % 2], out_hbm.at[at, :], store_sem.at[tile % 2]).wait()

    amplitude, noise = feat_ref[3:4, :], feat_ref[4:5, :]
    base = amplitude * amplitude + noise
    total = jnp.sum(taken[blocks]) + jnp.sum(base)
    resid_ref[...] += jnp.concatenate(
        [base[:, t * BLOCK : (t + 1) * BLOCK] for t in range(local_rows // BLOCK)], axis=0
    )
    lanes = lax.broadcasted_iota(jnp.int32, sums_ref.shape, 1)
    sums = jnp.zeros(sums_ref.shape, jnp.float32)
    for b in range(blocks):
        total = total - jnp.sum(taken[b])
        sums = jnp.where(lanes == b, total, sums)
    sums_ref[...] = sums


def broadcast_over(value, axes, count):
    copies = jnp.broadcast_to(value[None], (count,) + value.shape)
    return lax.all_to_all(copies, axes, 0, 0, tiled=True)


def local(locations, amplitude, noise, covariates, pivot_owner, pivot_offset):
    device_id = lax.axis_index(AXES)
    core = lax.axis_index("c")
    blocks_total, block_width = pivot_owner.shape
    pivots = blocks_total * block_width
    cov_width = covariates.shape[1]
    half = cov_width // 2
    local_rows = locations.shape[1]
    sizes = [lax.axis_size(name) for name in AXES]
    devices = sizes[0] * sizes[1] * sizes[2] * sizes[3]
    slots = CAP * blocks_total
    column = sizes[0] * sizes[3]
    planes = sizes[1] * sizes[2]

    same = pivot_owner[:, :, None] == pivot_owner[:, None, :]
    before = lax.iota(jnp.int32, block_width)[None, :] < lax.iota(jnp.int32, block_width)[:, None]
    rank = jnp.sum(jnp.where(same & before[None], 1, 0), axis=2)
    slot = (rank + CAP * lax.iota(jnp.int32, blocks_total)[:, None]).reshape(-1)
    owner = pivot_owner.reshape(-1)
    offset = pivot_offset.reshape(-1)
    here = (owner == device_id)[None, :] & (slot[None, :] == lax.iota(jnp.int32, slots)[:, None])
    my_offset = jnp.sum(jnp.where(here, offset[None, :], 0), axis=1)
    features = jnp.concatenate(
        [
            covariates[my_offset],
            locations[:, my_offset].T,
            amplitude[my_offset][:, None],
            noise[my_offset][:, None],
            jnp.zeros((slots, 123), jnp.float32),
        ],
        axis=1,
    )

    gathered = broadcast_over(features, ("z", "c"), column)
    gathered = gathered.reshape(column, blocks_total, CAP, -1).transpose(1, 0, 2, 3)
    gathered = gathered.reshape(column * slots, -1)
    cov_half = jnp.where(core == 0, gathered[:, :half], gathered[:, half:cov_width])
    message = jnp.concatenate([cov_half, gathered[:, cov_width : cov_width + 8].T], axis=0)
    mine = broadcast_over(message, ("x", "y"), planes)
    other = lax.ppermute(mine, "c", [(0, 1), (1, 0)])

    own_c = pivot_owner % sizes[3]
    chip = pivot_owner // sizes[3]
    place = (chip % planes) * (column * CAP) + ((chip // planes) * sizes[3] + own_c) * CAP + rank
    match = jnp.where(owner == device_id, offset, -1)[None, :]
    feat = jnp.concatenate(
        [locations, amplitude[None], noise[None], jnp.zeros((3, local_rows), jnp.float32)], axis=0
    )
    vmem = pl.BlockSpec(memory_space=pltpu.VMEM)
    hbm = pl.BlockSpec(memory_space=pl.ANY)
    factor, resid, sums = pl.pallas_call(
        main_kernel,
        out_shape=(
            jax.ShapeDtypeStruct((local_rows, pivots), jnp.float32),
            jax.ShapeDtypeStruct((local_rows // BLOCK, BLOCK), jnp.float32),
            jax.ShapeDtypeStruct((devices, BLOCK), jnp.float32),
        ),
        in_specs=[vmem, vmem, vmem, vmem, pl.BlockSpec(memory_space=pltpu.SMEM), vmem, hbm],
        out_specs=(hbm, vmem, vmem),
        scratch_shapes=[
            pltpu.VMEM((local_rows, cov_width), jnp.float32),
            pltpu.VMEM((pivots, cov_width), jnp.float32),
            pltpu.VMEM((SUB, pivots), jnp.float32),
            pltpu.VMEM((pivots, pivots), jnp.float32),
            pltpu.VMEM((BLOCK, pivots), jnp.float32),
            pltpu.VMEM((local_rows, SUB), jnp.float32),
            pltpu.VMEM((2, TILE, pivots), jnp.float32),
            pltpu.SemaphoreType.DMA,
            pltpu.SemaphoreType.DMA((2,)),
        ],
        compiler_params=pltpu.CompilerParams(vmem_limit_bytes=40 << 20),
        name="factor_rows",
    )(mine, other, place.T, match, core[None].astype(jnp.int32), feat, covariates)

    all_sums = lax.all_to_all(sums, AXES, 0, 0, tiled=True)
    mean_residual = jnp.sum(all_sums, axis=0)[:blocks_total] / float(local_rows * devices)
    weights = resid.reshape(-1) / mean_residual[blocks_total - 1]
    return (factor, weights, mean_residual)


def solution(mesh):
    named = Mesh(mesh.devices.reshape(8, 4, 4, 2), AXES)
    return jax.shard_map(
        local,
        mesh=named,
        in_specs=(P(None, AXES), P(AXES), P(AXES), P(AXES, None), P(), P()),
        out_specs=(P(AXES, None), P(AXES), P()),
        check_vma=False,
    )
```

profile of v0, /device:TPU:1, one launch (start us, length us, event | category | flops | bytes accessed | tf_op | source)
XLA Modules:
  0.0 126.9 jit_solution(17712176184186976039)
XLA Ops:
  0.7 0.7 broadcast_compare_fusion.1
  1.4 0.8 copy.81
  2.1 0.1 copy.94
  2.3 1.0 select_reduce_fusion
  3.3 0.8 copy.99
  4.1 0.1 add_select_fusion.2
  4.2 0.1 copy.96
  4.3 0.1 copy.82
  4.4 0.1 copy.97
  4.5 0.1 add_add_fusion
  4.5 0.8 select_reduce_fusion.1
  5.4 1.3 %gather_fusion.3 = f32[8]{0:T(128)S(1)} fusion(f32[2048]{0:T(1024)} %param.8, s32[1024]{0:T(1024)S(1)} %pad_clamp_fusion), kind=kCustom, calls=%fused_computation.3 | custom fusion | bytes 96 | tf_op jit(solution)/shard_map/gather | solution.py:310
  6.7 1.3 %gather_fusion.2 = f32[8]{0:T(128)S(1)} fusion(f32[2048]{0:T(1024)} %param.7, s32[1024]{0:T(1024)S(1)} %pad_clamp_fusion), kind=kCustom, calls=%fused_computation.2 | custom fusion | bytes 96 | tf_op jit(solution)/shard_map/gather | solution.py:309
  8.1 0.1 copy.84
  8.1 0.1 copy.85
  8.2 2.2 %gather_fusion = f32[8,256]{1,0:T(8,128)S(1)} fusion(f32[2048,256]{1,0:T(8,128)} %cov_hbm.1, s32[1024]{0:T(1024)S(1)} %pad_clamp_fusion), kind=kCustom, calls=%fused_computation | custom fusion | bytes 16416 | tf_op jit(solution)/shard_map/gather | solution.py:307
  10.4 1.1 copy.83
  11.5 0.6 gather_fusion.1
  12.1 0.1 concatenate.9
  12.2 0.7 broadcast_in_dim.78
  12.9 10.0 %all-to-all-start = ((f32[16,8,384]{2,1,0:T(8,128)}), f32[16,8,384]{2,1,0:T(8,128)S(1)}, u32[]{:S(2)}, u32[]{:S(2)}) async-start(f32[16,8,384]{2,1,0:T(8,128)} %broadcast_in_dim.78), calls=%async_computation | async-start | bytes 393216 | tf_op jit(solution)/shard_map/all_to_all | solution.py:280
  22.8 10.3 %all-to-all-done = f32[16,8,384]{2,1,0:T(8,128)S(1)} async-done(((f32[16,8,384]{2,1,0:T(8,128)}), f32[16,8,384]{2,1,0:T(8,128)S(1)}, u32[]{:S(2)}, u32[]{:S(2)}) %all-to-all-start) | async-done | bytes 196640 | tf_op jit(solution)/shard_map/all_to_all | solution.py:280
  33.2 0.1 copy.87
  33.3 0.1 reshape.96
  33.5 0.0 copy-start.1
  33.5 0.0 copy-start.2
  33.5 0.0 copy-start.3
  33.5 0.0 copy-start
  33.6 0.1 broadcast_in_dim.79
  33.7 24.5 %all_to_all.19.mine_ref = f32[16,136,128]{2,1,0:T(8,128)S(1)} all-to-all(f32[16,136,128]{2,1,0:T(8,128)S(1)} %broadcast_in_dim.79), channel_id=1, replica_groups=mesh['z'=8,'x'=4,'y'=4,'c'=2] {'x','y'}, dimensions={0} | all-to-all | bytes 2228224 | tf_op jit(solution)/shard_map/all_to_all | solution.py:280
  58.2 1.0 collective-permute-start
  59.2 0.1 copy.100
  59.2 0.1 copy.98
  59.4 0.1 pad.3.clone
  59.5 0.0 copy-done.1
  59.5 0.0 copy-done.2
  59.5 0.0 copy-done.3
  59.5 0.1 maximum_maximum_fusion.feat_ref
  59.5 2.2 %collective-permute-done.other_ref = f32[16,136,128]{2,1,0:T(8,128)} collective-permute-done((f32[16,136,128]{2,1,0:T(8,128)S(1)}, f32[16,136,128]{2,1,0:T(8,128)}, u32[]{:S(2)}, u32[]{:S(2)}) %collective-permute-start) | collective-permute-done | bytes 1114144 | tf_op jit(solution)/shard_map/ppermute | solution.py:322
  61.7 0.0 copy-done
  61.7 44.8 %factor_rows.1 = (f32[2048,512]{1,0:T(8,128)}, f32[16,128]{1,0:T(8,128)S(1)}, f32[256,128]{1,0:T(8,128)S(1)}) custom-call(f32[16,136,128]{2,1,0:T(8,128)S(1)} %all_to_all.19.mine_ref, f32[16,136,128]{2,1,0:T(8,128)} %collective-permute-done.other_ref, s32[128,4]{1,0:T(8,128)S(1)} %bitcast.26, s32[1,512]{1,0:T(1,128)S(1)} %bitcast.28, s32[1]{0:T(128)} %bitcast.12.core_ref, ...), custom_call_target="tpu_custom_call" | custom-call | tf_op jit(solution)/shard_map/factor_rows/pallas_call | solution.py:333
  106.5 18.2 %all_to_all.20 = f32[256,1,128]{2,1,0:T(1,128)S(1)} all-to-all(f32[256,1,128]{2,1,0:T(1,128)S(1)} %bitcast.27), channel_id=1, replica_groups=mesh['z'=8,'x'=4,'y'=4,'c'=2] {'z','x','y','c'}, dimensions={0} | all-to-all | bytes 262144 | tf_op jit(solution)/shard_map/all_to_all | solution.py:357
  124.7 0.3 reduce_sum.32
  125.0 0.0 copy-start.4
  125.0 0.6 slice.19
  125.6 1.2 divide_bitcast_fusion
  126.9 0.0 copy-done.4
  (12 shorter events, 0.2 us)
Async XLA Ops:
  12.9 20.3 %all-to-all-start = ((f32[16,8,384]{2,1,0:T(8,128)}), f32[16,8,384]{2,1,0:T(8,128)S(1)}, u32[]{:S(2)}, u32[]{:S(2)}) async-start(f32[16,8,384]{2,1,0:T(8,128)} %broadcast_in_dim.78), calls=%async_computation | async-start | bytes 393216 | tf_op jit(solution)/shard_map/all_to_all | solution.py:280
  33.5 26.0 %copy-start.1 = (f32[2048]{0:T(1024)S(1)}, f32[2048]{0:T(1024)}, u32[]{:S(2)}) copy-start(f32[2048]{0:T(1024)} %param.7) | copy-start | bytes 24580
  33.5 26.0 %copy-start.2 = (f32[2048]{0:T(1024)S(1)}, f32[2048]{0:T(1024)}, u32[]{:S(2)}) copy-start(f32[2048]{0:T(1024)} %param.8) | copy-start | bytes 24580
  33.5 26.0 %copy-start.3 = (f32[3,2048]{1,0:T(4,128)S(1)}, f32[3,2048]{1,0:T(4,128)}, u32[]{:S(2)}) copy-start(f32[3,2048]{1,0:T(4,128)} %param.6) | copy-start | bytes 73732
  33.5 28.2 %copy-start = (f32[2048,256]{1,0:T(8,128)S(1)}, f32[2048,256]{1,0:T(8,128)}, u32[]{:S(2)}) copy-start(f32[2048,256]{1,0:T(8,128)} %cov_hbm.1) | copy-start | bytes 6291460
  58.2 3.5 %collective-permute-start = (f32[16,136,128]{2,1,0:T(8,128)S(1)}, f32[16,136,128]{2,1,0:T(8,128)}, u32[]{:S(2)}, u32[]{:S(2)}) collective-permute-start(f32[16,136,128]{2,1,0:T(8,128)S(1)} %all_to_all.19.mine_ref), channel_id=1, source_target_pairs={{0,1},{1,0},{2,3},{3,2},{4,5},{5,4},{6,7},{7,6},{8,9},{9,8},{10,11... | collective-permute-start | bytes 3342344 | tf_op jit(solution)/shard_map/ppermute | solution.py:322
  125.0 1.9 %copy-start.4 = (f32[4]{0:T(128)}, f32[4]{0:T(128)S(1)}, u32[]{:S(2)}) copy-start(f32[4]{0:T(128)S(1)} %slice_multiply_fusion) | copy-start | bytes 52
where the time goes:
time: 127 us
  Pallas kernels  44.8 us (35%)
  blocking collectives  42.7 us (34%)
  waiting for transfers between devices  12.5 us (10%)
  starting transfers between devices  11 us (9%)
  local copies, waits for them, and re-layouts  10.8 us (9%)
  other arithmetic  4.38 us (3%)
    pallas_call x1, Pallas kernels, local(): pl.pallas_call(main_kernel, out_shape=(jax.ShapeDtypeStruct((local_rows,...  44.8 us
    all_to_all x1, blocking collectives, broadcast_over(): return lax.all_to_all(copies, axes, 0, 0, tiled=True)  24.5 us
    all_to_all x1, blocking collectives, local(): all_sums = lax.all_to_all(sums, AXES, 0, 0, tiled=True)  18.2 us
    all_to_all x1, waiting for transfers between devices, broadcast_over(): return lax.all_to_all(copies, axes, 0, 0, tiled=True)  10.3 us
    all_to_all x1, starting transfers between devices, broadcast_over(): return lax.all_to_all(copies, axes, 0, 0, tiled=True)  9.98 us
    unnamed x13, local copies, waits for them, and re-layouts  2.73 us
  transfers between devices with their start and end apart: 2, of which 2 were waited for; matrix products, arithmetic and copies ran while one was open for 0% of the time, Pallas kernels for 0%

commit v1 on v0

v1 whole, which is shorter than its diff:
```python
import jax
import jax.numpy as jnp
from jax import lax
from jax.experimental import pallas as pl
from jax.experimental.pallas import tpu as pltpu
from jax.sharding import Mesh
from jax.sharding import PartitionSpec as P

LENGTH_SCALE = 0.3
CAP = 2
AXES = ("z", "x", "y", "c")
HIGHEST = lax.Precision.HIGHEST
BLOCK = 128
PANEL = 16
SUB = 8
TILE = 256
FEW = 56


def dot(left, right, dims):
    return lax.dot_general(
        left, right, (dims, ((), ())), precision=HIGHEST, preferred_element_type=jnp.float32
    )


def panel_inverse(low, high):
    sub = lax.broadcasted_iota(jnp.int32, (SUB, BLOCK), 0)
    low, high = list(low), list(high)
    root_low = jnp.zeros((SUB, BLOCK), jnp.float32)
    root_high = root_low
    for k in range(PANEL):
        if k < SUB:
            pivot = jnp.broadcast_to(low[k][k : k + 1, :], (SUB, BLOCK))
            inverse = pl.reciprocal(pivot, approx=True)
            take_low = jnp.where(sub > k, low[k], 0.0) * inverse
            take_high = high[k] * inverse
            across = high[k]
            root_low = jnp.where(sub == k, lax.rsqrt(pivot), root_low)
            for j in range(PANEL):
                if j < SUB and j != k:
                    entry = low[j][k : k + 1, :]
                    low[j] = low[j] - take_low * entry
                    high[j] = high[j] - take_high * entry
                elif j >= SUB:
                    high[j] = high[j] - take_high * across[j - SUB : j - SUB + 1, :]
            low[k] = jnp.where(sub == k, 1.0, -take_low)
            high[k] = -take_high
        else:
            s = k - SUB
            pivot = jnp.broadcast_to(high[k][s : s + 1, :], (SUB, BLOCK))
            inverse = pl.reciprocal(pivot, approx=True)
            take_high = jnp.where(sub > s, high[k], 0.0) * inverse
            root_high = jnp.where(sub == s, lax.rsqrt(pivot), root_high)
            for j in range(PANEL):
                if j != k:
                    high[j] = high[j] - take_high * high[j][s : s + 1, :]
            high[k] = jnp.where(sub == s, 1.0, -take_high)
    return [low[j] * root_low for j in range(SUB)], [high[j] * root_high for j in range(PANEL)]


def tree_sum(terms):
    while len(terms) > 1:
        pairs = [terms[i] + terms[i + 1] for i in range(0, len(terms) - 1, 2)]
        terms = pairs + terms[2 * len(pairs) :]
    return terms[0]


def block_inverse(rows):
    lane = lax.broadcasted_iota(jnp.int32, (SUB, BLOCK), 1)
    sub = lax.broadcasted_iota(jnp.int32, (SUB, BLOCK), 0)
    rows = list(rows)
    out = [None] * len(rows)
    for panel in range(BLOCK // PANEL):
        first = PANEL * panel
        at = 2 * panel

        def splat(piece, j):
            return jnp.broadcast_to(piece[:, first + j : first + j + 1], (SUB, BLOCK))

        rest = range(at + 2, len(rows))
        near, far = rest[:2], rest[2:]
        low = [splat(rows[at], j) for j in range(SUB)]
        high = [splat(rows[at + 1], j) for j in range(PANEL)]
        coef = {r: [splat(rows[r], j) for j in range(PANEL)] for r in near}
        inv_low, inv_high = panel_inverse(low, high)
        in_panel = (lane >= first) & (lane < first + PANEL)
        top = jnp.where(in_panel, jnp.where(lane - first == sub, 1.0, 0.0), rows[at])
        bottom = jnp.where(in_panel, jnp.where(lane - first - SUB == sub, 1.0, 0.0), rows[at + 1])
        entries = [top[j : j + 1, :] for j in range(SUB)] + [bottom[j : j + 1, :] for j in range(SUB)]
        new_low = tree_sum([inv_low[j] * entries[j] for j in range(SUB)])
        new_high = tree_sum([inv_high[j] * entries[j] for j in range(PANEL)])
        out[at] = jnp.where(lane <= first + sub, new_low, 0.0)
        out[at + 1] = jnp.where(lane <= first + SUB + sub, new_high, 0.0)
        if len(near):
            weights = []
            for j in range(PANEL):
                term = inv_high[j] * new_high
                if j < SUB:
                    term = term + inv_low[j] * new_low
                weights.append(jnp.sum(term, axis=0, keepdims=True))
            for r in near:
                piece = jnp.where(in_panel, 0.0, rows[r])
                for j in range(PANEL):
                    piece = piece - coef[r][j] * weights[j]
                rows[r] = piece
        if len(far):
            spread = [jnp.zeros((size, BLOCK), jnp.float32) for size in (first, BLOCK - first - PANEL)]
            spread = ([spread[0]] if first else []) + weights + [spread[1]]
            change = dot(
                jnp.concatenate([rows[r] for r in far], axis=0),
                jnp.concatenate(spread, axis=0),
                ((1,), (0,)),
            )
            for i, r in enumerate(far):
                rows[r] = jnp.where(in_panel, 0.0, rows[r]) - change[SUB * i : SUB * (i + 1)]
    return out


def parts_of(value):
    high = value.astype(jnp.bfloat16)
    rest = value - high.astype(jnp.float32)
    middle = rest.astype(jnp.bfloat16)
    low = (rest - middle.astype(jnp.float32)).astype(jnp.bfloat16)
    return high, middle, low


def product(left, right, dims):
    return lax.dot_general(left, right, (dims, ((), ())), preferred_element_type=jnp.float32)


def dot_parts(left, right, dims):
    high, middle, low = left
    other_high, other_middle, other_low = right
    one = jnp.concatenate([low, high, middle, middle, high, high], axis=dims[0][0])
    two = jnp.concatenate(
        [other_high, other_low, other_middle, other_high, other_middle, other_high], axis=dims[1][0]
    )
    return product(one, two, dims)


def pick_rows(pick, value, dims):
    high, middle, low = parts_of(value)
    return product(pick, high, dims) + product(pick, middle, dims) + product(pick, low, dims)


def matern(cols, rows, col_scale, row_scale):
    dist_sq = None
    for axis_id in range(3):
        offset = cols[axis_id] - rows[axis_id]
        dist_sq = offset * offset if dist_sq is None else dist_sq + offset * offset
    scaled = dist_sq * lax.rsqrt(jnp.maximum(dist_sq, 1e-30))
    shape_term = (1.0 + scaled + dist_sq * (1.0 / 3.0)) * jnp.exp(-scaled)
    return col_scale * row_scale * shape_term


def prep_kernel(
    me_ref,
    owner_hbm,
    offset_hbm,
    points_hbm,
    amp_hbm,
    noise_hbm,
    cov_hbm,
    keep_ref,
    send_ref,
    owner_ref,
    offset_ref,
    points_ref,
    amp_ref,
    noise_ref,
    rows_ref,
    sem,
    load_sem,
):
    pairs = (
        (owner_hbm, owner_ref),
        (offset_hbm, offset_ref),
        (points_hbm, points_ref),
        (amp_hbm, amp_ref),
        (noise_hbm, noise_ref),
    )
    loads = [pltpu.make_async_copy(*pair, load_sem.at[i]) for i, pair in enumerate(pairs)]
    for load in loads:
        load.start()
    me = me_ref[0]
    core = lax.rem(me, 2)
    blocks, width = owner_ref.shape
    slots = CAP * blocks
    for load in loads:
        load.wait()
    lane = lax.broadcasted_iota(jnp.int32, (blocks, width), 1).astype(jnp.float32)
    block = lax.broadcasted_iota(jnp.int32, (blocks, width), 0)
    mine = owner_ref[...] == me
    offset = offset_ref[...].astype(jnp.float32)
    first = jnp.min(jnp.where(mine, lane, 1e4), axis=1, keepdims=True)
    last = jnp.max(jnp.where(mine, lane, -1.0), axis=1, keepdims=True)
    chosen = [jnp.where(mine & (lane == at), offset, 0.0) for at in (first, last)]
    copies = []
    slot_row = lax.broadcasted_iota(jnp.int32, (slots, 1), 0)
    offsets = jnp.zeros((slots, 1), jnp.int32)
    for s in range(slots):
        value = jnp.sum(jnp.where(block == s // CAP, chosen[s % CAP], 0.0)).astype(jnp.int32)
        copy = pltpu.make_async_copy(cov_hbm.at[pl.ds(value, 1), :], rows_ref.at[pl.ds(s, 1), :], sem.at[s])
        copy.start()
        copies.append(copy)
        offsets = jnp.where(slot_row == s, value, offsets)
    local_rows = points_ref.shape[1]
    hit = lax.broadcasted_iota(jnp.int32, (slots, local_rows), 1) == offsets
    sources = [points_ref[i : i + 1, :] for i in range(3)] + [amp_ref[...], noise_ref[...]]
    sub = lax.broadcasted_iota(jnp.int32, (SUB, BLOCK), 0)
    diagonal = sub == lax.broadcasted_iota(jnp.int32, (SUB, BLOCK), 1)
    scalars = jnp.zeros((SUB, BLOCK), jnp.float32)
    for i, source in enumerate(sources):
        column = jnp.sum(jnp.where(hit, source, 0.0), axis=1, keepdims=True)
        line = jnp.sum(jnp.where(diagonal, column, 0.0), axis=0, keepdims=True)
        scalars = jnp.where(sub == i, line, scalars)
    for copy in copies:
        copy.wait()
    half = rows_ref.shape[1] // 2
    left, right = rows_ref[:, :half], rows_ref[:, half:]
    keep_ref[:slots, :] = jnp.where(core == 0, left, right)
    send_ref[:slots, :] = jnp.where(core == 0, right, left)
    keep_ref[slots:, :] = scalars
    send_ref[slots:, :] = scalars


def pair_kernel(me_ref, keep_ref, got_ref, out_ref):
    core = lax.rem(me_ref[0], 2)
    keep, got = keep_ref[...], got_ref[...]
    one = jnp.where(core == 0, keep, got)
    two = jnp.where(core == 0, got, keep)
    lane = lax.broadcasted_iota(jnp.int32, (SUB, BLOCK), 1)
    scalars = jnp.where(lane < SUB, one[SUB:], pltpu.roll(two[SUB:], SUB, 1))
    for i in range(out_ref.shape[0]):
        out_ref[i, :SUB] = one[:SUB]
        out_ref[i, SUB : 2 * SUB] = two[:SUB]
        out_ref[i, 2 * SUB :] = scalars


def aux_kernel(
    me_ref,
    owner_ref,
    offset_ref,
    points_ref,
    amp_ref,
    noise_ref,
    cov_ref,
    high_ref,
    middle_ref,
    low_ref,
    feat_ref,
    base_ref,
    info_ref,
    match_ref,
    comb_ref,
    most_ref,
):
    me = me_ref[0]
    blocks, width = owner_ref.shape
    local_rows, cov_width = cov_ref.shape
    half = cov_width // 2
    owner = owner_ref[...]
    padded = jnp.concatenate([owner, jnp.zeros((SUB - blocks, width), jnp.int32)], axis=0)
    owner_t = padded.astype(jnp.float32).T.astype(jnp.int32)
    sub = lax.broadcasted_iota(jnp.int32, (width, width), 0)
    lane = lax.broadcasted_iota(jnp.int32, (width, width), 1)
    xy = (owner >> 1) & 15
    xy_t = (owner_t >> 1) & 15
    my_xy = lax.rem(lax.div(me, 2), 16)
    seats = []
    candidates = []
    infos = []
    for b in range(blocks):
        count = jnp.zeros((1, width), jnp.float32)
        for earlier in range(b + 1):
            same = xy_t[:, earlier : earlier + 1] == xy[b : b + 1, :]
            if earlier == b:
                same = same & (sub < lane)
            count = count + jnp.sum(jnp.where(same, 1.0, 0.0), axis=0, keepdims=True)
        twin = (owner_t[:, b : b + 1] == owner[b : b + 1, :]) & (sub < lane)
        rank = jnp.sum(jnp.where(twin, 1.0, 0.0), axis=0, keepdims=True).astype(jnp.int32)
        count = count.astype(jnp.int32)
        row = owner[b : b + 1, :]
        seats.append(jnp.where(xy[b : b + 1, :] == my_xy, count, -1))
        candidates.append((row >> 5) * 16 + (row & 1) * SUB + CAP * b + rank)
        infos.append(count)
    info_ref[:blocks, :] = xy.astype(jnp.float32)
    counts = jnp.concatenate(infos, axis=0).astype(jnp.float32)
    info_ref[blocks:, :] = counts
    most_ref[0] = jnp.max(counts).astype(jnp.int32) + 1
    match = jnp.where(owner == me, offset_ref[...], -1)
    match_ref[...] = jnp.concatenate([match[b : b + 1, :] for b in range(blocks)], axis=1)
    seat = jnp.concatenate(seats, axis=1)
    candidate = jnp.concatenate(candidates, axis=1)
    ids = lax.broadcasted_iota(jnp.int32, (BLOCK, blocks * width), 0)
    seat_hit = (ids == seat).astype(jnp.float32).astype(jnp.bfloat16)
    candidate_hit = (ids == candidate).astype(jnp.float32).astype(jnp.bfloat16)
    comb_ref[...] = product(seat_hit, candidate_hit, ((1,), (1,)))

    feat_ref[:3, :] = points_ref[...]
    feat_ref[3:4, :] = amp_ref[...]
    feat_ref[4:5, :] = noise_ref[...]
    feat_ref[5:, :] = jnp.zeros((3, local_rows), jnp.float32)
    diagonal = sub == lane

    def step(t, carry):
        at = pl.ds(pl.multiple_of(t * BLOCK, BLOCK), BLOCK)
        cov = cov_ref[at, :]
        high, middle, low = parts_of(cov)
        high_ref[at, :] = high
        middle_ref[at, :] = middle
        low_ref[at, :] = low
        squares = cov * cov
        line = jnp.sum(squares[:, :half] + squares[:, half:], axis=1, keepdims=True)
        total = jnp.sum(jnp.where(diagonal, line, 0.0), axis=0, keepdims=True)
        amplitude = amp_ref[:, at]
        base_ref[pl.ds(t, 1), :] = amplitude * amplitude + noise_ref[:, at] + total
        return carry

    lax.fori_loop(0, local_rows // BLOCK, step, 0)


def seat_kernel(comb_ref, got_ref, out_ref):
    chips = got_ref.shape[0]
    per_chip = got_ref.shape[1] - SUB
    seats = out_ref.shape[1] - SUB
    comb = comb_ref[...].astype(jnp.bfloat16)
    rows = jnp.concatenate([got_ref[z, :per_chip, :] for z in range(chips)], axis=0)
    packed = pick_rows(comb[: -(-seats // 16) * 16], rows, ((1,), (0,)))[:seats]
    lane = lax.broadcasted_iota(jnp.int32, (SUB, BLOCK), 1)
    scalars = jnp.zeros((SUB, BLOCK), jnp.float32)
    for z in range(chips):
        piece = got_ref[z, per_chip:, :]
        piece = pltpu.roll(piece, z * per_chip, 1) if z else piece
        scalars = jnp.where(lane // per_chip == z, piece, scalars)
    high, middle, low = parts_of(scalars)
    dims = ((1,), (1,))
    seated = product(high, comb, dims) + product(middle, comb, dims) + product(low, comb, dims)
    for i in range(out_ref.shape[0]):
        out_ref[i, :seats, :] = packed
        out_ref[i, seats:, :] = seated


def main_kernel(
    me_ref,
    mine_ref,
    other_ref,
    info_ref,
    match_ref,
    feat_ref,
    base_ref,
    high_hbm,
    middle_hbm,
    low_hbm,
    out_hbm,
    resid_ref,
    sums_ref,
    cov_high,
    cov_middle,
    cov_low,
    table_high,
    table_middle,
    table_low,
    kernel_high,
    kernel_middle,
    kernel_low,
    scal_ref,
    z_ref,
    r_ref,
    col_ref,
    tile_ref,
    load_sem,
    store_sem,
):
    core = lax.rem(me_ref[0], 2)
    pivots = z_ref.shape[0]
    local_rows, cov_width = cov_high.shape
    planes, plane_rows, half = mine_ref.shape
    seats = plane_rows - SUB
    blocks = pivots // BLOCK
    loads = [
        pltpu.make_async_copy(source, target, load_sem.at[i])
        for i, (source, target) in enumerate(
            ((high_hbm, cov_high), (middle_hbm, cov_middle), (low_hbm, cov_low))
        )
    ]
    for load in loads:
        load.start()
    nt = ((1,), (1,))

    scale = (5.0**0.5) / LENGTH_SCALE
    candidates = planes * plane_rows
    mine = mine_ref[...].reshape(candidates, half)
    other = other_ref[...].reshape(candidates, half)
    both = jnp.concatenate([jnp.where(core == 0, mine, other), jnp.where(core == 0, other, mine)], axis=1)
    both_parts = parts_of(both)
    packed = BLOCK // plane_rows if BLOCK % plane_rows == 0 else 1
    stride = BLOCK // packed
    lane = lax.broadcasted_iota(jnp.int32, (SUB, BLOCK), 1)
    lines = []
    for q in range(planes // packed):
        line = mine_ref[q * packed, seats:, :]
        for t in range(1, packed):
            piece = pltpu.roll(mine_ref[q * packed + t, seats:, :], t * stride, 1)
            line = jnp.where(lane // stride == t, piece, line)
        lines.append(line)
    line_parts = parts_of(jnp.concatenate(lines, axis=1))
    info_t = info_ref[...].T
    for b in range(blocks):
        here = pl.ds(b * BLOCK, BLOCK)
        xy, seat = info_t[:, b : b + 1], info_t[:, blocks + b : blocks + b + 1]
        place = (xy * plane_rows + seat).astype(jnp.int32)
        ids = lax.broadcasted_iota(jnp.int32, (BLOCK, candidates), 1)
        pick = (ids == place).astype(jnp.float32).astype(jnp.bfloat16)
        for part, table in zip(both_parts, (table_high, table_middle, table_low)):
            table[here, :] = product(pick, part, ((1,), (0,))).astype(jnp.bfloat16)
        if packed * plane_rows == BLOCK:
            line_pick = pick
        else:
            place = (xy * stride + seat).astype(jnp.int32)
            ids = lax.broadcasted_iota(jnp.int32, (BLOCK, planes * stride), 1)
            line_pick = (ids == place).astype(jnp.float32).astype(jnp.bfloat16)
        scal_ref[:, here] = (
            product(line_parts[0], line_pick, nt)
            + product(line_parts[1], line_pick, nt)
            + product(line_parts[2], line_pick, nt)
        )

    for t in range(local_rows // BLOCK):
        at = pl.ds(t * BLOCK, BLOCK)
        col_ref[at, :] = feat_ref[:, at].T
    piv = scal_ref[...]
    piv_rows = [piv[i : i + 1, :] * scale for i in range(3)]
    piv_scale, piv_noise = piv[3:4, :], piv[4:5, :]

    for b in range(blocks):
        here = pl.ds(b * BLOCK, BLOCK)
        right = slice(b * BLOCK, pivots)
        cols = scal_ref[:, here].T
        piece = matern(
            [cols[:, i : i + 1] * scale for i in range(3)],
            [row[:, right] for row in piv_rows],
            cols[:, 3:4],
            piv_scale[:, right],
        )
        same = lax.broadcasted_iota(jnp.int32, (BLOCK, 1), 0) == lax.broadcasted_iota(
            jnp.int32, (1, pivots - b * BLOCK), 1
        )
        piece = piece + jnp.where(same, piv_noise[:, right], 0.0)
        left_parts = [table[here, :] for table in (table_high, table_middle, table_low)]
        right_parts = [table[right, :] for table in (table_high, table_middle, table_low)]
        z_ref[here, right] = piece + dot_parts(left_parts, right_parts, nt)
        if b:
            z_ref[here, : b * BLOCK] = jnp.zeros((BLOCK, b * BLOCK), jnp.float32)
    for load in loads:
        load.wait()
    match = match_ref[...]

    def kernel_tile(t):
        at = pl.ds(pl.multiple_of(t * TILE, TILE), TILE)
        cols = col_ref[at, :]
        kernel = matern([cols[:, i : i + 1] * scale for i in range(3)], piv_rows, cols[:, 3:4], piv_scale)
        row_ids = lax.broadcasted_iota(jnp.int32, (TILE, 1), 0) + t * TILE
        kernel = kernel + jnp.where(row_ids == match, cols[:, 4:5], 0.0)
        cov = [part[at, :] for part in (cov_high, cov_middle, cov_low)]
        kernel = kernel + dot_parts(cov, (table_high[...], table_middle[...], table_low[...]), nt)
        for part, target in zip(parts_of(kernel), (kernel_high, kernel_middle, kernel_low)):
            target[at, :] = part

    per_step = local_rows // TILE // blocks

    def step(b, carry):
        at = pl.ds(pl.multiple_of(b * BLOCK, BLOCK), BLOCK)
        pieces = [
            z_ref[pl.ds(pl.multiple_of(b * BLOCK + SUB * i, SUB), SUB), at]
            for i in range(BLOCK // SUB)
        ]
        inverse = jnp.concatenate(block_inverse(pieces), axis=0)
        for i in range(per_step):
            kernel_tile(b * per_step + i)
        r_ref[...] = dot(inverse, z_ref[at, :], ((1,), (0,)))
        r_ref[:, at] = inverse
        z_ref[:, at] = jnp.zeros((pivots, BLOCK), jnp.float32)
        row = r_ref[...]
        row_parts = parts_of(row)
        for later in range(1, blocks):
            there = slice(later * BLOCK, (later + 1) * BLOCK)

            @pl.when(later > b)
            def _():
                coef = [part[:, there] for part in row_parts]
                z_ref[there, :] -= dot_parts(coef, row_parts, ((0,), (0,)))

        z_ref[at, :] = row
        return carry

    lax.fori_loop(0, blocks, step, 0)

    diagonal = lax.broadcasted_iota(jnp.int32, (BLOCK, BLOCK), 0) == lax.broadcasted_iota(
        jnp.int32, (BLOCK, BLOCK), 1
    )
    left = pivots // 2
    half_tiles = TILE // BLOCK
    tiles = local_rows // TILE
    inverse_parts = parts_of(z_ref[...])
    for part, target in zip(inverse_parts, (table_high, table_middle, table_low)):
        target[:, :] = part[:, :left]
    late = [part[left:, left:] for part in inverse_parts]

    def tile_step(t, taken):
        at = pl.ds(pl.multiple_of(t * TILE, TILE), TILE)
        slot = lax.rem(t, 2)

        @pl.when(t >= 2)
        def _():
            pltpu.make_async_copy(tile_ref.at[slot], out_hbm.at[at, :], store_sem.at[slot]).wait()

        kernels = [part[at, :] for part in (kernel_high, kernel_middle, kernel_low)]
        early = [part[:, :left] for part in kernels]
        first = dot_parts(early, [table[:left, :] for table in (table_high, table_middle, table_low)], nt)
        second = dot_parts(early, [table[left:, :] for table in (table_high, table_middle, table_low)], nt)
        second = second + dot_parts([part[:, left:] for part in kernels], late, nt)
        tile_ref[slot, :, :left] = first
        tile_ref[slot, :, left:] = second
        pltpu.make_async_copy(tile_ref.at[slot], out_hbm.at[at, :], store_sem.at[slot]).start()
        total = jnp.zeros((TILE, BLOCK), jnp.float32)
        new_taken = []
        for b in range(blocks):
            source = first if b * BLOCK < left else second
            piece = source[:, (b * BLOCK) % left : (b * BLOCK) % left + BLOCK]
            square = piece * piece
            total = total + square
            new_taken.append(taken[b] + jnp.sum(square.reshape(TILE // SUB, SUB, BLOCK), axis=0))
        line = jnp.sum(total, axis=1, keepdims=True)
        for h in range(half_tiles):
            spread = jnp.where(diagonal, line[h * BLOCK : (h + 1) * BLOCK, :], 0.0)
            where = pl.ds(t * half_tiles + h, 1)
            resid_ref[where, :] = base_ref[where, :] - jnp.sum(spread, axis=0, keepdims=True)
        return tuple(new_taken)

    zero = jnp.zeros((SUB, BLOCK), jnp.float32)
    taken = lax.fori_loop(0, tiles, tile_step, (zero,) * blocks)
    for tile in (tiles - 2, tiles - 1):
        at = pl.ds(tile * TILE, TILE)
        pltpu.make_async_copy(tile_ref.at[tile % 2], out_hbm.at[at, :], store_sem.at[tile % 2]).wait()

    total = jnp.sum(base_ref[...])
    lanes = lax.broadcasted_iota(jnp.int32, sums_ref.shape, 1)
    sums = jnp.zeros(sums_ref.shape, jnp.float32)
    for b in range(blocks):
        total = total - jnp.sum(taken[b])
        sums = jnp.where(lanes == b, total, sums)
    sums_ref[...] = sums


def last_kernel(sums_ref, resid_ref, weights_ref, mean_ref):
    devices, _, width = sums_ref.shape
    rows = resid_ref.shape[0] * resid_ref.shape[1] * devices
    total = jnp.sum(sums_ref[...].reshape(devices, width), axis=0, keepdims=True)
    mean = total * (1.0 / rows)
    count = mean_ref.shape[1]
    mean_ref[...] = mean[:, :count]
    weights_ref[...] = resid_ref[...] / mean[:, count - 1 : count]


def shape(dims, dtype=jnp.float32):
    return jax.ShapeDtypeStruct(dims, dtype)


VMEM = pl.BlockSpec(memory_space=pltpu.VMEM)
SMEM = pl.BlockSpec(memory_space=pltpu.SMEM)
ANY = pl.BlockSpec(memory_space=pl.ANY)
PARAMS = pltpu.CompilerParams(vmem_limit_bytes=40 << 20)


def prep(me, owner, offset, points, amp, noise, cov):
    rows = 2 * CAP * owner.shape[0]
    return pl.pallas_call(
        prep_kernel,
        out_shape=(shape((rows, BLOCK)), shape((rows, BLOCK))),
        in_specs=[SMEM] + [ANY] * 6,
        out_specs=(VMEM, VMEM),
        scratch_shapes=[pltpu.VMEM(value.shape, value.dtype) for value in (owner, offset, points, amp, noise)]
        + [
            pltpu.VMEM((rows // 2, cov.shape[1]), jnp.float32),
            pltpu.SemaphoreType.DMA((rows // 2,)),
            pltpu.SemaphoreType.DMA((5,)),
        ],
        compiler_params=pltpu.CompilerParams(vmem_limit_bytes=60 << 20),
        name="prep",
    )(me, owner, offset, points, amp, noise, cov)


def pair(me, keep, got, copies):
    return pl.pallas_call(
        pair_kernel,
        out_shape=shape((copies, 24, BLOCK)),
        in_specs=[SMEM, VMEM, VMEM],
        out_specs=VMEM,
        compiler_params=PARAMS,
        name="pair",
    )(me, keep, got)


def aux(me, owner, offset, points, amp, noise, cov):
    rows, width = cov.shape
    return pl.pallas_call(
        aux_kernel,
        out_shape=(
            shape((rows, width), jnp.bfloat16),
            shape((rows, width), jnp.bfloat16),
            shape((rows, width), jnp.bfloat16),
            shape((SUB, rows)),
            shape((rows // BLOCK, BLOCK)),
            shape((SUB, BLOCK)),
            shape((1, owner.size), jnp.int32),
            shape((BLOCK, BLOCK)),
            shape((1,), jnp.int32),
        ),
        in_specs=[SMEM] + [VMEM] * 6,
        out_specs=(VMEM,) * 8 + (SMEM,),
        compiler_params=PARAMS,
        cost_estimate=pl.CostEstimate(flops=10**8, bytes_accessed=6 << 20, transcendentals=0),
        name="aux",
    )(me, owner, offset, points, amp, noise, cov)


def seat(comb, got, copies, seats):
    return pl.pallas_call(
        seat_kernel,
        out_shape=shape((copies, seats + SUB, BLOCK)),
        in_specs=[VMEM, VMEM],
        out_specs=VMEM,
        compiler_params=PARAMS,
        name="seat",
    )(comb, got)


def main(me, mine, other, info, match, feat, base, high, middle, low, devices):
    rows, width = high.shape
    pivots = match.shape[1]
    bf = jnp.bfloat16
    return pl.pallas_call(
        main_kernel,
        out_shape=(shape((rows, pivots)), shape((rows // BLOCK, BLOCK)), shape((devices, BLOCK))),
        in_specs=[SMEM] + [VMEM] * 6 + [ANY] * 3,
        out_specs=(ANY, VMEM, VMEM),
        scratch_shapes=[pltpu.VMEM((rows, width), bf)] * 3
        + [pltpu.VMEM((pivots, width), bf)] * 3
        + [pltpu.VMEM((rows, pivots), bf)] * 3
        + [
            pltpu.VMEM((SUB, pivots), jnp.float32),
            pltpu.VMEM((pivots, pivots), jnp.float32),
            pltpu.VMEM((BLOCK, pivots), jnp.float32),
            pltpu.VMEM((rows, SUB), jnp.float32),
            pltpu.VMEM((2, TILE, pivots), jnp.float32),
            pltpu.SemaphoreType.DMA((3,)),
            pltpu.SemaphoreType.DMA((2,)),
        ],
        compiler_params=PARAMS,
        name="factor_rows",
    )(me, mine, other, info, match, feat, base, high, middle, low)


def last(sums, resid, blocks):
    return pl.pallas_call(
        last_kernel,
        out_shape=(shape(resid.shape), shape((1, blocks))),
        in_specs=[VMEM, VMEM],
        out_specs=(VMEM, VMEM),
        compiler_params=PARAMS,
        name="last",
    )(sums, resid)


def local(locations, amplitude, noise, covariates, pivot_owner, pivot_offset):
    me = lax.axis_index(AXES).astype(jnp.int32)[None]
    blocks = pivot_owner.shape[0]
    sizes = [lax.axis_size(name) for name in AXES]
    devices = sizes[0] * sizes[1] * sizes[2] * sizes[3]
    swap = [(0, 1), (1, 0)]
    amp, nugget = amplitude[None], noise[None]
    args = (me, pivot_owner, pivot_offset, locations, amp, nugget, covariates)

    keep, send = prep(*args)
    got = lax.ppermute(send, "c", swap)
    column = lax.all_to_all(pair(me, keep, got, sizes[0]), "z", 0, 0, tiled=True)
    high, middle, low, feat, base, info, match, comb, most = aux(*args)

    def rest(seats):
        def run(column, comb, info, match, feat, base, high, middle, low):
            message = seat(comb, column, sizes[1] * sizes[2], seats)
            mine = lax.all_to_all(message, ("x", "y"), 0, 0, tiled=True)
            other = lax.ppermute(mine, "c", swap)
            return main(me, mine, other, info, match, feat, base, high, middle, low, devices)

        return run

    operands = (column, comb, info, match, feat, base, high, middle, low)
    if FEW:
        factor, resid, sums = lax.cond(most[0] <= FEW, rest(FEW), rest(BLOCK), *operands)
    else:
        factor, resid, sums = rest(BLOCK)(*operands)
    all_sums = lax.all_to_all(sums[:, None, :], AXES, 0, 0, tiled=True)
    weights, mean_residual = last(all_sums, resid, blocks)
    return (factor, weights.reshape(-1), mean_residual.reshape(-1))


def solution(mesh):
    named = Mesh(mesh.devices.reshape(8, 4, 4, 2), AXES)
    return jax.shard_map(
        local,
        mesh=named,
        in_specs=(P(None, AXES), P(AXES), P(AXES), P(AXES, None), P(), P()),
        out_specs=(P(AXES, None), P(AXES), P()),
        check_vma=False,
    )
```

time: 127 us -> 96 us (0.76)
  local copies, waits for them, and re-layouts: 10.8 us -> 0.73 us
  blocking collectives: 42.7 us -> 35.3 us
  waiting for transfers between devices: 12.5 us -> 5.61 us
  Pallas kernels: 44.8 us -> 39.5 us
  other arithmetic: 4.38 us -> 0 us
  starting transfers between devices: 11 us -> 13 us
    all_to_all x2, blocking collectives: 42.7 us -> 35.3 us  [the longest x1 19.4 us: local(): all_sums = lax.all_to_all(sums[:, None, :], AXES, 0, 0, tiled=True)]
    all_to_all x1, waiting for transfers between devices: 10.3 us -> 3.03 us  [local(): lax.all_to_all(pair(me, keep, got, sizes[0]), 'z', 0, 0, tiled=True)]
    ppermute x1 -> x2, starting transfers between devices: 1 us -> 6.59 us  [the longest x1 3.34 us: local(): got = lax.ppermute(send, 'c', swap)]
    gather x4 -> x0, local copies, waits for them, and re-layouts: 5.4 us -> none  [the longest x1 2.16 us: local(): covariates[my_offset]]
    pallas_call x1 -> x6, Pallas kernels: 44.8 us -> 39.5 us  [the longest x1 31.3 us: main(): pl.pallas_call(main_kernel, out_shape=(shape((rows, pivots)), shape((rows...]
    all_to_all x1, starting transfers between devices: 9.98 us -> 6.44 us  [local(): lax.all_to_all(pair(me, keep, got, sizes[0]), 'z', 0, 0, tiled=True)]
    reduce_sum x3 -> x0, other arithmetic: 2.11 us -> none  [the longest x1 1 us: local(): rank = jnp.sum(jnp.where(same & before[None], 1, 0), axis=2)]
    unnamed x13 -> x14, local copies, waits for them, and re-layouts: 2.73 us -> 0.72 us
  transfers between devices with their start and end apart: 2 -> 3, of which waited for: 2 -> 3; matrix products, arithmetic and copies ran while one was open for 0% -> 0% of each run, Pallas kernels for 0% -> 4%
where the time goes in v1:
time: 96 us; the launch traced here: 95.6 us
  Pallas kernels  39.5 us (41%)
  blocking collectives  35.3 us (37%)
  starting transfers between devices  13 us (14%)
  waiting for transfers between devices  5.61 us (6%)
  between operations  1.41 us (1%)
    pallas_call x1, Pallas kernels, main(): pl.pallas_call(main_kernel, out_shape=(shape((rows, pivots)), shape((rows...  31.3 us
    all_to_all x1, blocking collectives, local(): all_sums = lax.all_to_all(sums[:, None, :], AXES, 0, 0, tiled=True)  19.4 us
    all_to_all x1, blocking collectives, run(): mine = lax.all_to_all(message, ('x', 'y'), 0, 0, tiled=True)  15.9 us
    all_to_all x1, starting transfers between devices, local(): lax.all_to_all(pair(me, keep, got, sizes[0]), 'z', 0, 0, tiled=True)  6.44 us
    pallas_call x1, Pallas kernels, aux(): pl.pallas_call(aux_kernel, out_shape=(shape((rows, width), jnp.bfloat16),...  3.71 us
    ppermute x1, starting transfers between devices, local(): got = lax.ppermute(send, 'c', swap)  3.34 us
    ppermute x1, starting transfers between devices, run(): other = lax.ppermute(mine, 'c', swap)  3.25 us
    all_to_all x1, waiting for transfers between devices, local(): lax.all_to_all(pair(me, keep, got, sizes[0]), 'z', 0, 0, tiled=True)  3.03 us
  transfers between devices with their start and end apart: 3, of which 3 were waited for; matrix products, arithmetic and copies ran while one was open for 0% of the time, Pallas kernels for 4%

profile of v1, /device:TPU:1, one launch (start us, length us, event | category | flops | bytes accessed | tf_op | source)
XLA Modules:
  0.0 95.6 jit_solution(9768070638407045755)
XLA Ops:
  0.6 0.0 copy-start.5
  0.6 0.0 copy-start.4
  0.7 0.0 copy-start
  0.7 0.0 copy-start.1
  0.7 0.0 copy-start.3
  0.7 0.0 copy-start.2
  0.7 2.8 %prep.1 = (f32[16,128]{1,0:T(8,128)}, f32[16,128]{1,0:T(8,128)}) custom-call(s32[1]{0:T(128)} %bitcast.me_ref, s32[4,128]{1,0:T(4,128)} %owner_hbm.1, s32[4,128]{1,0:T(4,128)} %offset_hbm.1, f32[3,2048]{1,0:T(4,128)} %points_hbm.1, f32[1,2048]{1,0:T(1,128)} %bitcast.7, f32[1,2048]{1,0:T(1,128)} %bitcast.9, f32[2048,256]{1,0:T(8,128)} %cov_hbm.1), custom_call_target="tpu_custom_call" | custom-call | tf_op jit(solution)/shard_map/prep/pallas_call | solution.py:578
  3.5 3.3 %collective-permute-start.2 = (f32[16,128]{1,0:T(8,128)}, f32[16,128]{1,0:T(8,128)S(1)}, u32[]{:S(2)}, u32[]{:S(2)}) collective-permute-start(f32[16,128]{1,0:T(8,128)} %get-tuple-element.82), channel_id=1, source_target_pairs={{0,1},{1,0},{2,3},{3,2},{4,5},{5,4},{6,7},{7,6},{8,9},{9,8},{10,11... | collective-permute-start | bytes 24584 | tf_op jit(solution)/shard_map/ppermute | solution.py:686
  6.8 1.0 %collective-permute-done.2.got_ref = f32[16,128]{1,0:T(8,128)S(1)} collective-permute-done((f32[16,128]{1,0:T(8,128)}, f32[16,128]{1,0:T(8,128)S(1)}, u32[]{:S(2)}, u32[]{:S(2)}) %collective-permute-start.2) | collective-permute-done | bytes 8224 | tf_op jit(solution)/shard_map/ppermute | solution.py:686
  7.8 0.0 copy-start.6
  7.8 0.7 copy-done.6
  8.5 0.7 pair.1
  9.3 6.4 %all-to-all-start.2 = ((f32[8,24,128]{2,1,0:T(8,128)}), f32[8,24,128]{2,1,0:T(8,128)S(1)}, u32[]{:S(2)}, u32[]{:S(2)}) async-start(f32[8,24,128]{2,1,0:T(8,128)} %pair.1), calls=%async_computation.2 | async-start | bytes 196608 | tf_op jit(solution)/shard_map/all_to_all | solution.py:687
  15.7 0.0 copy-done.5
  15.7 0.0 copy-done.4
  15.7 0.0 copy-done
  15.7 0.0 copy-done.1
  15.7 0.0 copy-done.3
  15.7 0.0 copy-done.2
  15.8 3.7 %aux.1 = (bf16[2048,256]{1,0:T(8,128)(2,1)S(1)}, bf16[2048,256]{1,0:T(8,128)(2,1)}, bf16[2048,256]{1,0:T(8,128)(2,1)}, f32[8,2048]{1,0:T(8,128)S(1)}, f32[16,128...) custom-call(s32[1]{0:T(128)} %bitcast.me_ref, ...), custom_call_target="tpu_custom_call" | custom-call | flops 100000000 | bytes 6291456 | tf_op jit(solution)/shard_map/aux/pallas_call | solution.py:607
  20.1 3.0 %all-to-all-done.2 = f32[8,24,128]{2,1,0:T(8,128)S(1)} async-done(((f32[8,24,128]{2,1,0:T(8,128)}), f32[8,24,128]{2,1,0:T(8,128)S(1)}, u32[]{:S(2)}, u32[]{:S(2)}) %all-to-all-start.2) | async-done | bytes 98336 | tf_op jit(solution)/shard_map/all_to_all | solution.py:687
  23.2 52.2 %conditional.1 = ((f32[2048,512]{1,0:T(8,128)}, f32[16,128]{1,0:T(8,128)S(1)}, f32[256,128]{1,0:T(8,128)S(1)})) conditional(s32[]{:T(128)} %bitcast.3, (f32[128,128]{1,0:T(8,128)S(1)}, f32[8,24,128]{2,1,0:T(8,128)S(1)}, s32[1]{0:T(128)}, f32[8,128]{1,0:T(8,128)S(1)}, s32[1,512]{1,0:T(1,128)S(1)}, /*index=5*/f32[8,2048]{1,0:T(8,128)S(1)}, ...), branch_computations={%region_0.0_spmd, %region_1.0_spmd} | conditional | bytes 15073384 | solution.py:701
  23.2 0.0 copy-start.8
  23.2 0.2 seat.3
  23.4 15.9 %all_to_all.19.mine_ref = f32[16,64,128]{2,1,0:T(8,128)S(1)} all-to-all(f32[16,64,128]{2,1,0:T(8,128)S(1)} %seat.3), channel_id=1, replica_groups=mesh['z'=8,'x'=4,'y'=4,'c'=2] {'x','y'}, dimensions={0} | all-to-all | bytes 1048576 | tf_op jit(solution)/shard_map/cond/branch_1_fun/all_to_all | solution.py:693
  39.3 3.2 %collective-permute-start.1 = (f32[16,64,128]{2,1,0:T(8,128)S(1)}, f32[16,64,128]{2,1,0:T(8,128)S(1)}, u32[]{:S(2)}, u32[]{:S(2)}) collective-permute-start(f32[16,64,128]{2,1,0:T(8,128)S(1)} %all_to_all.19.mine_ref), channel_id=1, source_target_pairs={{0,1},{1,0},{2,3},{3,2},{4,5},{5,4},{6,7},{7,6},{8,9},{9,8},{10,11... | collective-permute-start | bytes 1572872 | tf_op jit(solution)/shard_map/cond/branch_1_fun/ppermute | solution.py:694
  42.5 1.5 %collective-permute-done.1.other_ref = f32[16,64,128]{2,1,0:T(8,128)S(1)} collective-permute-done((f32[16,64,128]{2,1,0:T(8,128)S(1)}, f32[16,64,128]{2,1,0:T(8,128)S(1)}, u32[]{:S(2)}, u32[]{:S(2)}) %collective-permute-start.1) | collective-permute-done | bytes 524320 | tf_op jit(solution)/shard_map/cond/branch_1_fun/ppermute | solution.py:694
  44.1 0.0 copy-done.8
  44.1 31.3 %factor_rows.3 = (f32[2048,512]{1,0:T(8,128)}, f32[16,128]{1,0:T(8,128)S(1)}, f32[256,128]{1,0:T(8,128)S(1)}) custom-call(s32[1]{0:T(128)} %get-tuple-element.50.me_ref, f32[16,64,128]{2,1,0:T(8,128)S(1)} %all_to_all.19.mine_ref, f32[16,64,128]{2,1,0:T(8,128)S(1)} %collective-permute-done.1.other_ref, f32[8,128]{1,0:T(8,128)S(1)} %get-tuple-element.53.info_ref, ...), custom_call_target="tpu_custom_call" | custom-call | tf_op jit(solution)/shard_map/cond/branch_1_fun/factor_rows/pallas_call | solution.py:643
  75.3 19.4 %all_to_all.20.sums_ref = f32[256,1,128]{2,1,0:T(1,128)S(1)} all-to-all(f32[256,1,128]{2,1,0:T(1,128)S(1)} %bitcast.11), channel_id=1, replica_groups=mesh['z'=8,'x'=4,'y'=4,'c'=2] {'z','x','y','c'}, dimensions={0} | all-to-all | bytes 262144 | tf_op jit(solution)/shard_map/all_to_all | solution.py:704
  94.8 0.8 last.1
Async XLA Ops:
  0.6 15.1 %copy-start.5 = (s32[4,128]{1,0:T(4,128)S(1)}, s32[4,128]{1,0:T(4,128)}, u32[]{:S(2)}) copy-start(s32[4,128]{1,0:T(4,128)} %offset_hbm.1) | copy-start | bytes 6148
  0.6 15.1 %copy-start.4 = (s32[4,128]{1,0:T(4,128)S(1)}, s32[4,128]{1,0:T(4,128)}, u32[]{:S(2)}) copy-start(s32[4,128]{1,0:T(4,128)} %owner_hbm.1) | copy-start | bytes 6148
  0.7 15.1 %copy-start = (f32[2048,256]{1,0:T(8,128)S(1)}, f32[2048,256]{1,0:T(8,128)}, u32[]{:S(2)}) copy-start(f32[2048,256]{1,0:T(8,128)} %cov_hbm.1) | copy-start | bytes 6291460
  0.7 15.1 %copy-start.1 = (f32[3,2048]{1,0:T(4,128)S(1)}, f32[3,2048]{1,0:T(4,128)}, u32[]{:S(2)}) copy-start(f32[3,2048]{1,0:T(4,128)} %points_hbm.1) | copy-start | bytes 73732
  0.7 15.1 %copy-start.3 = (f32[2048]{0:T(1024)S(1)}, f32[2048]{0:T(1024)}, u32[]{:S(2)}) copy-start(f32[2048]{0:T(1024)} %param.10) | copy-start | bytes 24580
  0.7 15.1 %copy-start.2 = (f32[2048]{0:T(1024)S(1)}, f32[2048]{0:T(1024)}, u32[]{:S(2)}) copy-start(f32[2048]{0:T(1024)} %param.9) | copy-start | bytes 24580
  3.5 4.4 %collective-permute-start.2 = (f32[16,128]{1,0:T(8,128)}, f32[16,128]{1,0:T(8,128)S(1)}, u32[]{:S(2)}, u32[]{:S(2)}) collective-permute-start(f32[16,128]{1,0:T(8,128)} %get-tuple-element.82), channel_id=1, source_target_pairs={{0,1},{1,0},{2,3},{3,2},{4,5},{5,4},{6,7},{7,6},{8,9},{9,8},{10,11... | collective-permute-start | bytes 24584 | tf_op jit(solution)/shard_map/ppermute | solution.py:686
  7.8 0.7 copy-start.6
  9.3 13.9 %all-to-all-start.2 = ((f32[8,24,128]{2,1,0:T(8,128)}), f32[8,24,128]{2,1,0:T(8,128)S(1)}, u32[]{:S(2)}, u32[]{:S(2)}) async-start(f32[8,24,128]{2,1,0:T(8,128)} %pair.1), calls=%async_computation.2 | async-start | bytes 196608 | tf_op jit(solution)/shard_map/all_to_all | solution.py:687
  23.2 20.9 %copy-start.8 = (bf16[2048,256]{1,0:T(8,128)(2,1)S(1)}, bf16[2048,256]{1,0:T(8,128)(2,1)}, u32[]{:S(2)}) copy-start(bf16[2048,256]{1,0:T(8,128)(2,1)} %get-tuple-element.58.middle_hbm) | copy-start | bytes 3145732 | tf_op jit(solution)/shard_map/cond
  39.3 4.8 %collective-permute-start.1 = (f32[16,64,128]{2,1,0:T(8,128)S(1)}, f32[16,64,128]{2,1,0:T(8,128)S(1)}, u32[]{:S(2)}, u32[]{:S(2)}) collective-permute-start(f32[16,64,128]{2,1,0:T(8,128)S(1)} %all_to_all.19.mine_ref), channel_id=1, source_target_pairs={{0,1},{1,0},{2,3},{3,2},{4,5},{5,4},{6,7},{7,6},{8,9},{9,8},{10,11... | collective-permute-start | bytes 1572872 | tf_op jit(solution)/shard_map/cond/branch_1_fun/ppermute | solution.py:694

commit v2 on v1

--- a/solution.py
+++ b/solution.py
@@ -15,6 +15,7 @@
 SUB = 8
 TILE = 256
 FEW = 56
+WIDE = 512
 
 
 def dot(left, right, dims):
@@ -161,8 +162,7 @@
     amp_hbm,
     noise_hbm,
     cov_hbm,
-    keep_ref,
-    send_ref,
+    out_ref,
     owner_ref,
     offset_ref,
     points_ref,
@@ -183,10 +183,9 @@
     for load in loads:
         load.start()
     me = me_ref[0]
-    core = lax.rem(me, 2)
     blocks, width = owner_ref.shape
     slots = CAP * blocks
-    for load in loads:
+    for load in loads[:2]:
         load.wait()
     lane = lax.broadcasted_iota(jnp.int32, (blocks, width), 1).astype(jnp.float32)
     block = lax.broadcasted_iota(jnp.int32, (blocks, width), 0)
@@ -204,6 +203,8 @@
         copy.start()
         copies.append(copy)
         offsets = jnp.where(slot_row == s, value, offsets)
+    for load in loads[2:]:
+        load.wait()
     local_rows = points_ref.shape[1]
     hit = lax.broadcasted_iota(jnp.int32, (slots, local_rows), 1) == offsets
     sources = [points_ref[i : i + 1, :] for i in range(3)] + [amp_ref[...], noise_ref[...]]
@@ -218,23 +219,10 @@
         copy.wait()
     half = rows_ref.shape[1] // 2
     left, right = rows_ref[:, :half], rows_ref[:, half:]
-    keep_ref[:slots, :] = jnp.where(core == 0, left, right)
-    send_ref[:slots, :] = jnp.where(core == 0, right, left)
-    keep_ref[slots:, :] = scalars
-    send_ref[slots:, :] = scalars
-
-
-def pair_kernel(me_ref, keep_ref, got_ref, out_ref):
-    core = lax.rem(me_ref[0], 2)
-    keep, got = keep_ref[...], got_ref[...]
-    one = jnp.where(core == 0, keep, got)
-    two = jnp.where(core == 0, got, keep)
-    lane = lax.broadcasted_iota(jnp.int32, (SUB, BLOCK), 1)
-    scalars = jnp.where(lane < SUB, one[SUB:], pltpu.roll(two[SUB:], SUB, 1))
     for i in range(out_ref.shape[0]):
-        out_ref[i, :SUB] = one[:SUB]
-        out_ref[i, SUB : 2 * SUB] = two[:SUB]
-        out_ref[i, 2 * SUB :] = scalars
+        out_ref[i, :slots, :] = left
+        out_ref[i, slots : 2 * slots, :] = right
+        out_ref[i, 2 * slots :, :] = scalars
 
 
 def aux_kernel(
@@ -320,19 +308,22 @@
     lax.fori_loop(0, local_rows // BLOCK, step, 0)
 
 
-def seat_kernel(comb_ref, got_ref, out_ref):
-    chips = got_ref.shape[0]
-    per_chip = got_ref.shape[1] - SUB
+def seat_kernel(me_ref, comb_ref, got_ref, out_ref):
+    core = lax.rem(me_ref[0], 2)
+    senders = got_ref.shape[0]
+    slots = (got_ref.shape[1] - SUB) // 2
     seats = out_ref.shape[1] - SUB
     comb = comb_ref[...].astype(jnp.bfloat16)
-    rows = jnp.concatenate([got_ref[z, :per_chip, :] for z in range(chips)], axis=0)
+    left = jnp.concatenate([got_ref[i, :slots, :] for i in range(senders)], axis=0)
+    right = jnp.concatenate([got_ref[i, slots : 2 * slots, :] for i in range(senders)], axis=0)
+    rows = jnp.where(core == 0, left, right)
     packed = pick_rows(comb[: -(-seats // 16) * 16], rows, ((1,), (0,)))[:seats]
     lane = lax.broadcasted_iota(jnp.int32, (SUB, BLOCK), 1)
     scalars = jnp.zeros((SUB, BLOCK), jnp.float32)
-    for z in range(chips):
-        piece = got_ref[z, per_chip:, :]
-        piece = pltpu.roll(piece, z * per_chip, 1) if z else piece
-        scalars = jnp.where(lane // per_chip == z, piece, scalars)
+    for i in range(senders):
+        piece = got_ref[i, 2 * slots :, :]
+        piece = pltpu.roll(piece, i * slots, 1) if i else piece
+        scalars = jnp.where(lane // slots == i, piece, scalars)
     high, middle, low = parts_of(scalars)
     dims = ((1,), (1,))
     seated = product(high, comb, dims) + product(middle, comb, dims) + product(low, comb, dims)
@@ -500,15 +491,15 @@
         jnp.int32, (BLOCK, BLOCK), 1
     )
     left = pivots // 2
-    half_tiles = TILE // BLOCK
-    tiles = local_rows // TILE
+    half_tiles = WIDE // BLOCK
+    tiles = local_rows // WIDE
     inverse_parts = parts_of(z_ref[...])
     for part, target in zip(inverse_parts, (table_high, table_middle, table_low)):
         target[:, :] = part[:, :left]
     late = [part[left:, left:] for part in inverse_parts]
 
     def tile_step(t, taken):
-        at = pl.ds(pl.multiple_of(t * TILE, TILE), TILE)
+        at = pl.ds(pl.multiple_of(t * WIDE, WIDE), WIDE)
         slot = lax.rem(t, 2)
 
         @pl.when(t >= 2)
@@ -523,14 +514,14 @@
         tile_ref[slot, :, :left] = first
         tile_ref[slot, :, left:] = second
         pltpu.make_async_copy(tile_ref.at[slot], out_hbm.at[at, :], store_sem.at[slot]).start()
-        total = jnp.zeros((TILE, BLOCK), jnp.float32)
+        total = jnp.zeros((WIDE, BLOCK), jnp.float32)
         new_taken = []
         for b in range(blocks):
             source = first if b * BLOCK < left else second
             piece = source[:, (b * BLOCK) % left : (b * BLOCK) % left + BLOCK]
             square = piece * piece
             total = total + square
-            new_taken.append(taken[b] + jnp.sum(square.reshape(TILE // SUB, SUB, BLOCK), axis=0))
+            new_taken.append(taken[b] + jnp.sum(square.reshape(WIDE // SUB, SUB, BLOCK), axis=0))
         line = jnp.sum(total, axis=1, keepdims=True)
         for h in range(half_tiles):
             spread = jnp.where(diagonal, line[h * BLOCK : (h + 1) * BLOCK, :], 0.0)
@@ -541,7 +532,7 @@
     zero = jnp.zeros((SUB, BLOCK), jnp.float32)
     taken = lax.fori_loop(0, tiles, tile_step, (zero,) * blocks)
     for tile in (tiles - 2, tiles - 1):
-        at = pl.ds(tile * TILE, TILE)
+        at = pl.ds(tile * WIDE, WIDE)
         pltpu.make_async_copy(tile_ref.at[tile % 2], out_hbm.at[at, :], store_sem.at[tile % 2]).wait()
 
     total = jnp.sum(base_ref[...])
@@ -573,33 +564,22 @@
 PARAMS = pltpu.CompilerParams(vmem_limit_bytes=40 << 20)
 
 
-def prep(me, owner, offset, points, amp, noise, cov):
-    rows = 2 * CAP * owner.shape[0]
+def prep(me, owner, offset, points, amp, noise, cov, copies):
+    slots = CAP * owner.shape[0]
     return pl.pallas_call(
         prep_kernel,
-        out_shape=(shape((rows, BLOCK)), shape((rows, BLOCK))),
+        out_shape=shape((copies, 2 * slots + SUB, BLOCK)),
         in_specs=[SMEM] + [ANY] * 6,
-        out_specs=(VMEM, VMEM),
+        out_specs=VMEM,
         scratch_shapes=[pltpu.VMEM(value.shape, value.dtype) for value in (owner, offset, points, amp, noise)]
         + [
-            pltpu.VMEM((rows // 2, cov.shape[1]), jnp.float32),
-            pltpu.SemaphoreType.DMA((rows // 2,)),
+            pltpu.VMEM((slots, cov.shape[1]), jnp.float32),
+            pltpu.SemaphoreType.DMA((slots,)),
             pltpu.SemaphoreType.DMA((5,)),
         ],
         compiler_params=pltpu.CompilerParams(vmem_limit_bytes=60 << 20),
         name="prep",
     )(me, owner, offset, points, amp, noise, cov)
-
-
-def pair(me, keep, got, copies):
-    return pl.pallas_call(
-        pair_kernel,
-        out_shape=shape((copies, 24, BLOCK)),
-        in_specs=[SMEM, VMEM, VMEM],
-        out_specs=VMEM,
-        compiler_params=PARAMS,
-        name="pair",
-    )(me, keep, got)
 
 
 def aux(me, owner, offset, points, amp, noise, cov):
@@ -625,15 +605,15 @@
     )(me, owner, offset, points, amp, noise, cov)
 
 
-def seat(comb, got, copies, seats):
+def seat(me, comb, got, copies, seats):
     return pl.pallas_call(
         seat_kernel,
         out_shape=shape((copies, seats + SUB, BLOCK)),
-        in_specs=[VMEM, VMEM],
+        in_specs=[SMEM, VMEM, VMEM],
         out_specs=VMEM,
         compiler_params=PARAMS,
         name="seat",
-    )(comb, got)
+    )(me, comb, got)
 
 
 def main(me, mine, other, info, match, feat, base, high, middle, low, devices):
@@ -653,7 +633,7 @@
             pltpu.VMEM((pivots, pivots), jnp.float32),
             pltpu.VMEM((BLOCK, pivots), jnp.float32),
             pltpu.VMEM((rows, SUB), jnp.float32),
-            pltpu.VMEM((2, TILE, pivots), jnp.float32),
+            pltpu.VMEM((2, WIDE, pivots), jnp.float32),
             pltpu.SemaphoreType.DMA((3,)),
             pltpu.SemaphoreType.DMA((2,)),
         ],
@@ -682,14 +662,12 @@
     amp, nugget = amplitude[None], noise[None]
     args = (me, pivot_owner, pivot_offset, locations, amp, nugget, covariates)
 
-    keep, send = prep(*args)
-    got = lax.ppermute(send, "c", swap)
-    column = lax.all_to_all(pair(me, keep, got, sizes[0]), "z", 0, 0, tiled=True)
+    column = lax.all_to_all(prep(*args, sizes[0] * sizes[3]), ("z", "c"), 0, 0, tiled=True)
     high, middle, low, feat, base, info, match, comb, most = aux(*args)
 
     def rest(seats):
         def run(column, comb, info, match, feat, base, high, middle, low):
-            message = seat(comb, column, sizes[1] * sizes[2], seats)
+            message = seat(me, comb, column, sizes[1] * sizes[2], seats)
             mine = lax.all_to_all(message, ("x", "y"), 0, 0, tiled=True)
             other = lax.ppermute(mine, "c", swap)
             return main(me, mine, other, info, match, feat, base, high, middle, low, devices)

time: 96 us -> 94.2 us (0.981)
  waiting for transfers between devices: 5.61 us -> 7.43 us
  Pallas kernels: 39.5 us -> 37.7 us
  starting transfers between devices: 13 us -> 11.4 us
    all_to_all x1, starting transfers between devices: 6.44 us -> 9.96 us  [local(): lax.all_to_all(prep(*args, sizes[0] * sizes[3]), ('z', 'c'), 0, 0, tiled=...]
    ppermute x1 -> x0, starting transfers between devices: 3.34 us -> none  [local(): got = lax.ppermute(send, 'c', swap)]
    all_to_all x1, waiting for transfers between devices: 3.03 us -> 5.9 us  [local(): lax.all_to_all(prep(*args, sizes[0] * sizes[3]), ('z', 'c'), 0, 0, tiled=...]
    all_to_all x1, blocking collectives: 15.9 us -> 17.8 us  [run(): mine = lax.all_to_all(message, ('x', 'y'), 0, 0, tiled=True)]
    ppermute x1, starting transfers between devices: 3.25 us -> 1.41 us  [run(): other = lax.ppermute(mine, 'c', swap)]
    all_to_all x1, blocking collectives: 19.4 us -> 18.2 us  [local(): all_sums = lax.all_to_all(sums[:, None, :], AXES, 0, 0, tiled=True)]
    ppermute x1 -> x0, waiting for transfers between devices: 1.04 us -> none  [local(): got = lax.ppermute(send, 'c', swap)]
    pallas_call x1, Pallas kernels: 31.3 us -> 30.3 us  [main(): pl.pallas_call(main_kernel, out_shape=(shape((rows, pivots)), shape((rows...]
  transfers between devices with their start and end apart: 3 -> 2, of which waited for: 3 -> 2; matrix products, arithmetic and copies ran while one was open for 0% -> 0% of each run, Pallas kernels for 4% -> 4%
where the time goes in v2:
time: 94.2 us; the launch traced here: 94 us
  Pallas kernels  37.7 us (40%)
  blocking collectives  36.1 us (38%)
  starting transfers between devices  11.4 us (12%)
  waiting for transfers between devices  7.43 us (8%)
  between operations  1.41 us (1%)
    pallas_call x1, Pallas kernels, main(): pl.pallas_call(main_kernel, out_shape=(shape((rows, pivots)), shape((rows...  30.3 us
    all_to_all x1, blocking collectives, local(): all_sums = lax.all_to_all(sums[:, None, :], AXES, 0, 0, tiled=True)  18.2 us
    all_to_all x1, blocking collectives, run(): mine = lax.all_to_all(message, ('x', 'y'), 0, 0, tiled=True)  17.8 us
    all_to_all x1, starting transfers between devices, local(): lax.all_to_all(prep(*args, sizes[0] * sizes[3]), ('z', 'c'), 0, 0, tiled=...  9.96 us
    all_to_all x1, waiting for transfers between devices, local(): lax.all_to_all(prep(*args, sizes[0] * sizes[3]), ('z', 'c'), 0, 0, tiled=...  5.9 us
    pallas_call x1, Pallas kernels, aux(): pl.pallas_call(aux_kernel, out_shape=(shape((rows, width), jnp.bfloat16),...  3.72 us
    pallas_call x1, Pallas kernels, prep(): pl.pallas_call(prep_kernel, out_shape=shape((copies, 2 * slots + SUB, BLO...  2.68 us
  transfers between devices with their start and end apart: 2, of which 2 were waited for; matrix products, arithmetic and copies ran while one was open for 0% of the time, Pallas kernels for 4%

profile of v2, /device:TPU:1, one launch (start us, length us, event | category | flops | bytes accessed | tf_op | source)
XLA Modules:
  0.0 94.0 jit_solution(18434923005287459412)
XLA Ops:
  0.6 0.0 copy-start.5
  0.6 0.0 copy-start.4
  0.7 0.0 copy-start
  0.7 0.0 copy-start.1
  0.7 0.0 copy-start.3
  0.7 0.0 copy-start.2
  0.7 2.7 %prep.1 = f32[16,24,128]{2,1,0:T(8,128)} custom-call(s32[1]{0:T(128)} %bitcast.me_ref, s32[4,128]{1,0:T(4,128)} %owner_hbm.1, s32[4,128]{1,0:T(4,128)} %offset_hbm.1, f32[3,2048]{1,0:T(4,128)} %points_hbm.1, f32[1,2048]{1,0:T(1,128)} %bitcast.7, f32[1,2048]{1,0:T(1,128)} %bitcast.9, f32[2048,256]{1,0:T(8,128)} %cov_hbm.1), custom_call_target="tpu_custom_call" | custom-call | tf_op jit(solution)/shard_map/prep/pallas_call | solution.py:569
  3.4 10.0 %all-to-all-start.2 = ((f32[16,24,128]{2,1,0:T(8,128)}), f32[16,24,128]{2,1,0:T(8,128)S(1)}, u32[]{:S(2)}, u32[]{:S(2)}) async-start(f32[16,24,128]{2,1,0:T(8,128)} %prep.1), calls=%async_computation.2 | async-start | bytes 393216 | tf_op jit(solution)/shard_map/all_to_all | solution.py:665
  13.3 0.0 copy-done.5
  13.3 0.0 copy-done.4
  13.4 0.0 copy-done
  13.4 0.0 copy-done.1
  13.4 0.0 copy-done.3
  13.4 0.0 copy-done.2
  13.4 3.7 %aux.1 = (bf16[2048,256]{1,0:T(8,128)(2,1)S(1)}, bf16[2048,256]{1,0:T(8,128)(2,1)}, bf16[2048,256]{1,0:T(8,128)(2,1)}, f32[8,2048]{1,0:T(8,128)S(1)}, f32[16,128...) custom-call(s32[1]{0:T(128)} %bitcast.me_ref, ...), custom_call_target="tpu_custom_call" | custom-call | flops 100000000 | bytes 6291456 | tf_op jit(solution)/shard_map/aux/pallas_call | solution.py:587
  17.8 5.9 %all-to-all-done.2 = f32[16,24,128]{2,1,0:T(8,128)S(1)} async-done(((f32[16,24,128]{2,1,0:T(8,128)}), f32[16,24,128]{2,1,0:T(8,128)S(1)}, u32[]{:S(2)}, u32[]{:S(2)}) %all-to-all-start.2) | async-done | bytes 196640 | tf_op jit(solution)/shard_map/all_to_all | solution.py:665
  23.7 51.3 %conditional.1 = ((f32[2048,512]{1,0:T(8,128)}, f32[16,128]{1,0:T(8,128)S(1)}, f32[256,128]{1,0:T(8,128)S(1)})) conditional(s32[]{:T(128)} %bitcast.3, (s32[1]{0:T(128)}, f32[128,128]{1,0:T(8,128)S(1)}, f32[16,24,128]{2,1,0:T(8,128)S(1)}, f32[8,128]{1,0:T(8,128)S(1)}, s32[1,512]{1,0:T(1,128)S(1)}, /*index=5*/f32[8,2048]{1,0:T(8,128)S(1)}, ...), branch_computations={%region_0.0_spmd, %region_1.0_spmd} | conditional | bytes 15073384 | solution.py:679
  23.7 0.0 copy-start.7
  23.7 0.2 seat.3
  23.9 17.8 %all_to_all.19.mine_ref = f32[16,64,128]{2,1,0:T(8,128)S(1)} all-to-all(f32[16,64,128]{2,1,0:T(8,128)S(1)} %seat.3), channel_id=1, replica_groups=mesh['z'=8,'x'=4,'y'=4,'c'=2] {'x','y'}, dimensions={0} | all-to-all | bytes 1048576 | tf_op jit(solution)/shard_map/cond/branch_1_fun/all_to_all | solution.py:671
  41.7 1.4 %collective-permute-start.1 = (f32[16,64,128]{2,1,0:T(8,128)S(1)}, f32[16,64,128]{2,1,0:T(8,128)S(1)}, u32[]{:S(2)}, u32[]{:S(2)}) collective-permute-start(f32[16,64,128]{2,1,0:T(8,128)S(1)} %all_to_all.19.mine_ref), channel_id=1, source_target_pairs={{0,1},{1,0},{2,3},{3,2},{4,5},{5,4},{6,7},{7,6},{8,9},{9,8},{10,11... | collective-permute-start | bytes 1572872 | tf_op jit(solution)/shard_map/cond/branch_1_fun/ppermute | solution.py:672
  43.1 1.5 %collective-permute-done.1.other_ref = f32[16,64,128]{2,1,0:T(8,128)S(1)} collective-permute-done((f32[16,64,128]{2,1,0:T(8,128)S(1)}, f32[16,64,128]{2,1,0:T(8,128)S(1)}, u32[]{:S(2)}, u32[]{:S(2)}) %collective-permute-start.1) | collective-permute-done | bytes 524320 | tf_op jit(solution)/shard_map/cond/branch_1_fun/ppermute | solution.py:672
  44.7 0.0 copy-done.7
  44.7 30.3 %factor_rows.3 = (f32[2048,512]{1,0:T(8,128)}, f32[16,128]{1,0:T(8,128)S(1)}, f32[256,128]{1,0:T(8,128)S(1)}) custom-call(s32[1]{0:T(128)} %get-tuple-element.50.me_ref, f32[16,64,128]{2,1,0:T(8,128)S(1)} %all_to_all.19.mine_ref, f32[16,64,128]{2,1,0:T(8,128)S(1)} %collective-permute-done.1.other_ref, f32[8,128]{1,0:T(8,128)S(1)} %get-tuple-element.53.info_ref, ...), custom_call_target="tpu_custom_call" | custom-call | tf_op jit(solution)/shard_map/cond/branch_1_fun/factor_rows/pallas_call | solution.py:623
  75.0 18.2 %all_to_all.20.sums_ref = f32[256,1,128]{2,1,0:T(1,128)S(1)} all-to-all(f32[256,1,128]{2,1,0:T(1,128)S(1)} %bitcast.11), channel_id=1, replica_groups=mesh['z'=8,'x'=4,'y'=4,'c'=2] {'z','x','y','c'}, dimensions={0} | all-to-all | bytes 262144 | tf_op jit(solution)/shard_map/all_to_all | solution.py:682
  93.2 0.8 last.1
Async XLA Ops:
  0.6 12.7 %copy-start.5 = (s32[4,128]{1,0:T(4,128)S(1)}, s32[4,128]{1,0:T(4,128)}, u32[]{:S(2)}) copy-start(s32[4,128]{1,0:T(4,128)} %offset_hbm.1) | copy-start | bytes 6148
  0.6 12.7 %copy-start.4 = (s32[4,128]{1,0:T(4,128)S(1)}, s32[4,128]{1,0:T(4,128)}, u32[]{:S(2)}) copy-start(s32[4,128]{1,0:T(4,128)} %owner_hbm.1) | copy-start | bytes 6148
  0.7 12.7 %copy-start = (f32[2048,256]{1,0:T(8,128)S(1)}, f32[2048,256]{1,0:T(8,128)}, u32[]{:S(2)}) copy-start(f32[2048,256]{1,0:T(8,128)} %cov_hbm.1) | copy-start | bytes 6291460
  0.7 12.7 %copy-start.1 = (f32[3,2048]{1,0:T(4,128)S(1)}, f32[3,2048]{1,0:T(4,128)}, u32[]{:S(2)}) copy-start(f32[3,2048]{1,0:T(4,128)} %points_hbm.1) | copy-start | bytes 73732
  0.7 12.7 %copy-start.3 = (f32[2048]{0:T(1024)S(1)}, f32[2048]{0:T(1024)}, u32[]{:S(2)}) copy-start(f32[2048]{0:T(1024)} %param.10) | copy-start | bytes 24580
  0.7 12.7 %copy-start.2 = (f32[2048]{0:T(1024)S(1)}, f32[2048]{0:T(1024)}, u32[]{:S(2)}) copy-start(f32[2048]{0:T(1024)} %param.9) | copy-start | bytes 24580
  3.4 20.3 %all-to-all-start.2 = ((f32[16,24,128]{2,1,0:T(8,128)}), f32[16,24,128]{2,1,0:T(8,128)S(1)}, u32[]{:S(2)}, u32[]{:S(2)}) async-start(f32[16,24,128]{2,1,0:T(8,128)} %prep.1), calls=%async_computation.2 | async-start | bytes 393216 | tf_op jit(solution)/shard_map/all_to_all | solution.py:665
  23.7 21.0 %copy-start.7 = (bf16[2048,256]{1,0:T(8,128)(2,1)S(1)}, bf16[2048,256]{1,0:T(8,128)(2,1)}, u32[]{:S(2)}) copy-start(bf16[2048,256]{1,0:T(8,128)(2,1)} %get-tuple-element.58.middle_hbm) | copy-start | bytes 3145732 | tf_op jit(solution)/shard_map/cond
  41.7 2.9 %collective-permute-start.1 = (f32[16,64,128]{2,1,0:T(8,128)S(1)}, f32[16,64,128]{2,1,0:T(8,128)S(1)}, u32[]{:S(2)}, u32[]{:S(2)}) collective-permute-start(f32[16,64,128]{2,1,0:T(8,128)S(1)} %all_to_all.19.mine_ref), channel_id=1, source_target_pairs={{0,1},{1,0},{2,3},{3,2},{4,5},{5,4},{6,7},{7,6},{8,9},{9,8},{10,11... | collective-permute-start | bytes 1572872 | tf_op jit(solution)/shard_map/cond/branch_1_fun/ppermute | solution.py:672

commit v3 on v2

--- a/solution.py
+++ b/solution.py
@@ -1,3 +1,5 @@
+import functools
+
 import jax
 import jax.numpy as jnp
 from jax import lax
@@ -16,6 +18,7 @@
 TILE = 256
 FEW = 56
 WIDE = 512
+LOG2E = 1.4426950408889634
 
 
 def dot(left, right, dims):
@@ -29,29 +32,36 @@
     low, high = list(low), list(high)
     root_low = jnp.zeros((SUB, BLOCK), jnp.float32)
     root_high = root_low
+
+    def entry(j, i):
+        piece = low[j][i : i + 1, :] if i < SUB else high[j][i - SUB : i - SUB + 1, :]
+        return jnp.broadcast_to(piece, (SUB, BLOCK))
+
+    pivot = entry(0, 0)
     for k in range(PANEL):
+        inverse = pl.reciprocal(pivot, approx=True)
+        root = lax.rsqrt(pivot)
+        if k + 1 < PANEL:
+            side = entry(k, k + 1)
+            pivot = entry(k + 1, k + 1) - (side * side) * inverse
         if k < SUB:
-            pivot = jnp.broadcast_to(low[k][k : k + 1, :], (SUB, BLOCK))
-            inverse = pl.reciprocal(pivot, approx=True)
             take_low = jnp.where(sub > k, low[k], 0.0) * inverse
             take_high = high[k] * inverse
             across = high[k]
-            root_low = jnp.where(sub == k, lax.rsqrt(pivot), root_low)
+            root_low = jnp.where(sub == k, root, root_low)
             for j in range(PANEL):
                 if j < SUB and j != k:
-                    entry = low[j][k : k + 1, :]
-                    low[j] = low[j] - take_low * entry
-                    high[j] = high[j] - take_high * entry
+                    line = low[j][k : k + 1, :]
+                    low[j] = low[j] - take_low * line
+                    high[j] = high[j] - take_high * line
                 elif j >= SUB:
                     high[j] = high[j] - take_high * across[j - SUB : j - SUB + 1, :]
             low[k] = jnp.where(sub == k, 1.0, -take_low)
             high[k] = -take_high
         else:
             s = k - SUB
-            pivot = jnp.broadcast_to(high[k][s : s + 1, :], (SUB, BLOCK))
-            inverse = pl.reciprocal(pivot, approx=True)
             take_high = jnp.where(sub > s, high[k], 0.0) * inverse
-            root_high = jnp.where(sub == s, lax.rsqrt(pivot), root_high)
+            root_high = jnp.where(sub == s, root, root_high)
             for j in range(PANEL):
                 if j != k:
                     high[j] = high[j] - take_high * high[j][s : s + 1, :]
@@ -105,13 +115,13 @@
                     piece = piece - coef[r][j] * weights[j]
                 rows[r] = piece
         if len(far):
-            spread = [jnp.zeros((size, BLOCK), jnp.float32) for size in (first, BLOCK - first - PANEL)]
-            spread = ([spread[0]] if first else []) + weights + [spread[1]]
-            change = dot(
-                jnp.concatenate([rows[r] for r in far], axis=0),
-                jnp.concatenate(spread, axis=0),
-                ((1,), (0,)),
-            )
+            spread = []
+            for part in parts_of(jnp.concatenate(weights, axis=0)):
+                above = [jnp.zeros((first, BLOCK), jnp.bfloat16)] if first else []
+                below = [jnp.zeros((BLOCK - first - PANEL, BLOCK), jnp.bfloat16)]
+                spread.append(jnp.concatenate(above + [part] + below, axis=0))
+            far_rows = parts_of(jnp.concatenate([rows[r] for r in far], axis=0))
+            change = dot_parts(far_rows, spread, ((1,), (0,)))
             for i, r in enumerate(far):
                 rows[r] = jnp.where(in_panel, 0.0, rows[r]) - change[SUB * i : SUB * (i + 1)]
     return out
@@ -241,6 +251,7 @@
     info_ref,
     match_ref,
     comb_ref,
+    left_ref,
     most_ref,
 ):
     me = me_ref[0]
@@ -290,6 +301,8 @@
     feat_ref[4:5, :] = noise_ref[...]
     feat_ref[5:, :] = jnp.zeros((3, local_rows), jnp.float32)
     diagonal = sub == lane
+    scale = (5.0**0.5) / LENGTH_SCALE
+    order = (0, 0, 1, 1, 0, 2)
 
     def step(t, carry):
         at = pl.ds(pl.multiple_of(t * BLOCK, BLOCK), BLOCK)
@@ -301,6 +314,13 @@
         squares = cov * cov
         line = jnp.sum(squares[:, :half] + squares[:, half:], axis=1, keepdims=True)
         total = jnp.sum(jnp.where(diagonal, line, 0.0), axis=0, keepdims=True)
+        points = (points_ref[:, at] - 0.5) * scale
+        point_parts = [part.astype(jnp.float32) for part in parts_of(points)]
+        length = jnp.sum(points * points, axis=0, keepdims=True)
+        lines = [point_parts[k][i : i + 1, :] for i in range(3) for k in order]
+        lines += [part.astype(jnp.float32) for part in parts_of(length)] + [jnp.ones((3, BLOCK), jnp.float32)]
+        lines.append(jnp.zeros((BLOCK - 6 * len(order) + 12, BLOCK), jnp.float32))
+        left_ref[at, :] = jnp.concatenate(lines, axis=0).T.astype(jnp.bfloat16)
         amplitude = amp_ref[:, at]
         base_ref[pl.ds(t, 1), :] = amplitude * amplitude + noise_ref[:, at] + total
         return carry
@@ -332,13 +352,73 @@
         out_ref[i, seats:, :] = seated
 
 
+def field_kernel(mine_ref, info_ref, match_ref, feat_ref, left_ref, scal_ref, field_ref, col_ref):
+    pivots = match_ref.shape[1]
+    local_rows = feat_ref.shape[1]
+    planes, plane_rows, _ = mine_ref.shape
+    seats = plane_rows - SUB
+    blocks = pivots // BLOCK
+    nt = ((1,), (1,))
+    packed = BLOCK // plane_rows if BLOCK % plane_rows == 0 else 1
+    stride = BLOCK // packed
+    lane = lax.broadcasted_iota(jnp.int32, (SUB, BLOCK), 1)
+    lines = []
+    for q in range(planes // packed):
+        line = mine_ref[q * packed, seats:, :]
+        for t in range(1, packed):
+            piece = pltpu.roll(mine_ref[q * packed + t, seats:, :], t * stride, 1)
+            line = jnp.where(lane // stride == t, piece, line)
+        lines.append(line)
+    line_parts = parts_of(jnp.concatenate(lines, axis=1))
+    info_t = info_ref[...].T
+    for b in range(blocks):
+        here = pl.ds(b * BLOCK, BLOCK)
+        xy, seat = info_t[:, b : b + 1], info_t[:, blocks + b : blocks + b + 1]
+        place = (xy * stride + seat).astype(jnp.int32)
+        ids = lax.broadcasted_iota(jnp.int32, (BLOCK, planes * stride), 1)
+        line_pick = (ids == place).astype(jnp.float32).astype(jnp.bfloat16)
+        scal_ref[:, here] = (
+            product(line_parts[0], line_pick, nt)
+            + product(line_parts[1], line_pick, nt)
+            + product(line_parts[2], line_pick, nt)
+        )
+    for t in range(local_rows // BLOCK):
+        at = pl.ds(t * BLOCK, BLOCK)
+        col_ref[at, :] = feat_ref[:, at].T
+    piv = scal_ref[...]
+    piv_scale = piv[3:4, :]
+    match = match_ref[...]
+
+    scale = (5.0**0.5) / LENGTH_SCALE
+    points = (piv[:3, :] - 0.5) * scale
+    length = jnp.sum(points * points, axis=0, keepdims=True)
+    point_parts = [part.astype(jnp.float32) * -2.0 for part in parts_of(points)]
+    lines = [point_parts[k][i : i + 1, :] for i in range(3) for k in (0, 1, 0, 1, 2, 0)]
+    lines += [jnp.ones((3, pivots), jnp.float32)] + [part.astype(jnp.float32) for part in parts_of(length)]
+    lines.append(jnp.zeros((BLOCK - 24, pivots), jnp.float32))
+    right = jnp.concatenate(lines, axis=0).astype(jnp.bfloat16)
+
+    def step(t, carry):
+        at = pl.ds(pl.multiple_of(t * WIDE, WIDE), WIDE)
+        cols = col_ref[at, :]
+        dist_sq = jnp.maximum(product(left_ref[at, :], right, ((1,), (0,))), 1e-30)
+        scaled = dist_sq * lax.rsqrt(dist_sq)
+        value = (1.0 + scaled + dist_sq * (1.0 / 3.0)) * jnp.exp2(scaled * -LOG2E)
+        value = cols[:, 3:4] * piv_scale * value
+        row_ids = lax.broadcasted_iota(jnp.int32, (WIDE, 1), 0) + t * WIDE
+        field_ref[at, :] = value + jnp.where(row_ids == match, cols[:, 4:5], 0.0)
+        return carry
+
+    lax.fori_loop(0, local_rows // WIDE, step, 0)
+
+
 def main_kernel(
     me_ref,
     mine_ref,
     other_ref,
     info_ref,
-    match_ref,
-    feat_ref,
+    scal_ref,
+    field_ref,
     base_ref,
     high_hbm,
     middle_hbm,
@@ -355,10 +435,8 @@
     kernel_high,
     kernel_middle,
     kernel_low,
-    scal_ref,
     z_ref,
     r_ref,
-    col_ref,
     tile_ref,
     load_sem,
     store_sem,
@@ -367,7 +445,6 @@
     pivots = z_ref.shape[0]
     local_rows, cov_width = cov_high.shape
     planes, plane_rows, half = mine_ref.shape
-    seats = plane_rows - SUB
     blocks = pivots // BLOCK
     loads = [
         pltpu.make_async_copy(source, target, load_sem.at[i])
@@ -385,17 +462,6 @@
     other = other_ref[...].reshape(candidates, half)
     both = jnp.concatenate([jnp.where(core == 0, mine, other), jnp.where(core == 0, other, mine)], axis=1)
     both_parts = parts_of(both)
-    packed = BLOCK // plane_rows if BLOCK % plane_rows == 0 else 1
-    stride = BLOCK // packed
-    lane = lax.broadcasted_iota(jnp.int32, (SUB, BLOCK), 1)
-    lines = []
-    for q in range(planes // packed):
-        line = mine_ref[q * packed, seats:, :]
-        for t in range(1, packed):
-            piece = pltpu.roll(mine_ref[q * packed + t, seats:, :], t * stride, 1)
-            line = jnp.where(lane // stride == t, piece, line)
-        lines.append(line)
-    line_parts = parts_of(jnp.concatenate(lines, axis=1))
     info_t = info_ref[...].T
     for b in range(blocks):
         here = pl.ds(b * BLOCK, BLOCK)
@@ -405,21 +471,7 @@
         pick = (ids == place).astype(jnp.float32).astype(jnp.bfloat16)
         for part, table in zip(both_parts, (table_high, table_middle, table_low)):
             table[here, :] = product(pick, part, ((1,), (0,))).astype(jnp.bfloat16)
-        if packed * plane_rows == BLOCK:
-            line_pick = pick
-        else:
-            place = (xy * stride + seat).astype(jnp.int32)
-            ids = lax.broadcasted_iota(jnp.int32, (BLOCK, planes * stride), 1)
-            line_pick = (ids == place).astype(jnp.float32).astype(jnp.bfloat16)
-        scal_ref[:, here] = (
-            product(line_parts[0], line_pick, nt)
-            + product(line_parts[1], line_pick, nt)
-            + product(line_parts[2], line_pick, nt)
-        )
-
-    for t in range(local_rows // BLOCK):
-        at = pl.ds(t * BLOCK, BLOCK)
-        col_ref[at, :] = feat_ref[:, at].T
+
     piv = scal_ref[...]
     piv_rows = [piv[i : i + 1, :] * scale for i in range(3)]
     piv_scale, piv_noise = piv[3:4, :], piv[4:5, :]
@@ -445,20 +497,14 @@
             z_ref[here, : b * BLOCK] = jnp.zeros((BLOCK, b * BLOCK), jnp.float32)
     for load in loads:
         load.wait()
-    match = match_ref[...]
-
     def kernel_tile(t):
-        at = pl.ds(pl.multiple_of(t * TILE, TILE), TILE)
-        cols = col_ref[at, :]
-        kernel = matern([cols[:, i : i + 1] * scale for i in range(3)], piv_rows, cols[:, 3:4], piv_scale)
-        row_ids = lax.broadcasted_iota(jnp.int32, (TILE, 1), 0) + t * TILE
-        kernel = kernel + jnp.where(row_ids == match, cols[:, 4:5], 0.0)
+        at = pl.ds(pl.multiple_of(t * WIDE, WIDE), WIDE)
         cov = [part[at, :] for part in (cov_high, cov_middle, cov_low)]
-        kernel = kernel + dot_parts(cov, (table_high[...], table_middle[...], table_low[...]), nt)
+        kernel = field_ref[at, :] + dot_parts(cov, (table_high[...], table_middle[...], table_low[...]), nt)
         for part, target in zip(parts_of(kernel), (kernel_high, kernel_middle, kernel_low)):
             target[at, :] = part
 
-    per_step = local_rows // TILE // blocks
+    per_step = local_rows // WIDE // blocks
 
     def step(b, carry):
         at = pl.ds(pl.multiple_of(b * BLOCK, BLOCK), BLOCK)
@@ -469,18 +515,17 @@
         inverse = jnp.concatenate(block_inverse(pieces), axis=0)
         for i in range(per_step):
             kernel_tile(b * per_step + i)
-        r_ref[...] = dot(inverse, z_ref[at, :], ((1,), (0,)))
+        r_ref[...] = dot_parts(parts_of(inverse), parts_of(z_ref[at, :]), ((1,), (0,)))
         r_ref[:, at] = inverse
         z_ref[:, at] = jnp.zeros((pivots, BLOCK), jnp.float32)
         row = r_ref[...]
-        row_parts = parts_of(row)
-        for later in range(1, blocks):
-            there = slice(later * BLOCK, (later + 1) * BLOCK)
-
-            @pl.when(later > b)
+        for s in range(blocks - 1):
+
+            @pl.when(b == s)
             def _():
-                coef = [part[:, there] for part in row_parts]
-                z_ref[there, :] -= dot_parts(coef, row_parts, ((0,), (0,)))
+                later = slice((s + 1) * BLOCK, pivots)
+                coef = parts_of(row[:, later].T)
+                z_ref[later, :] -= dot_parts(coef, parts_of(row), ((1,), (0,)))
 
         z_ref[at, :] = row
         return carry
@@ -544,9 +589,8 @@
     sums_ref[...] = sums
 
 
-def last_kernel(sums_ref, resid_ref, weights_ref, mean_ref):
+def last_kernel(sums_ref, resid_ref, weights_ref, mean_ref, *, rows):
     devices, _, width = sums_ref.shape
-    rows = resid_ref.shape[0] * resid_ref.shape[1] * devices
     total = jnp.sum(sums_ref[...].reshape(devices, width), axis=0, keepdims=True)
     mean = total * (1.0 / rows)
     count = mean_ref.shape[1]
@@ -595,10 +639,11 @@
             shape((SUB, BLOCK)),
             shape((1, owner.size), jnp.int32),
             shape((BLOCK, BLOCK)),
+            shape((rows, BLOCK), jnp.bfloat16),
             shape((1,), jnp.int32),
         ),
         in_specs=[SMEM] + [VMEM] * 6,
-        out_specs=(VMEM,) * 8 + (SMEM,),
+        out_specs=(VMEM,) * 9 + (SMEM,),
         compiler_params=PARAMS,
         cost_estimate=pl.CostEstimate(flops=10**8, bytes_accessed=6 << 20, transcendentals=0),
         name="aux",
@@ -616,9 +661,23 @@
     )(me, comb, got)
 
 
-def main(me, mine, other, info, match, feat, base, high, middle, low, devices):
+def field(mine, info, match, feat, left):
+    pivots, rows = match.shape[1], feat.shape[1]
+    return pl.pallas_call(
+        field_kernel,
+        out_shape=(shape((SUB, pivots)), shape((rows, pivots))),
+        in_specs=[VMEM] * 5,
+        out_specs=(VMEM, VMEM),
+        scratch_shapes=[pltpu.VMEM((rows, SUB), jnp.float32)],
+        compiler_params=PARAMS,
+        cost_estimate=pl.CostEstimate(flops=10**8, bytes_accessed=6 << 20, transcendentals=0),
+        name="field",
+    )(mine, info, match, feat, left)
+
+
+def main(me, mine, other, info, scal, local_field, base, high, middle, low, devices):
     rows, width = high.shape
-    pivots = match.shape[1]
+    pivots = scal.shape[1]
     bf = jnp.bfloat16
     return pl.pallas_call(
         main_kernel,
@@ -629,22 +688,20 @@
         + [pltpu.VMEM((pivots, width), bf)] * 3
         + [pltpu.VMEM((rows, pivots), bf)] * 3
         + [
-            pltpu.VMEM((SUB, pivots), jnp.float32),
             pltpu.VMEM((pivots, pivots), jnp.float32),
             pltpu.VMEM((BLOCK, pivots), jnp.float32),
-            pltpu.VMEM((rows, SUB), jnp.float32),
             pltpu.VMEM((2, WIDE, pivots), jnp.float32),
             pltpu.SemaphoreType.DMA((3,)),
             pltpu.SemaphoreType.DMA((2,)),
         ],
         compiler_params=PARAMS,
         name="factor_rows",
-    )(me, mine, other, info, match, feat, base, high, middle, low)
-
-
-def last(sums, resid, blocks):
+    )(me, mine, other, info, scal, local_field, base, high, middle, low)
+
+
+def last(sums, resid, blocks, rows):
     return pl.pallas_call(
-        last_kernel,
+        functools.partial(last_kernel, rows=rows),
         out_shape=(shape(resid.shape), shape((1, blocks))),
         in_specs=[VMEM, VMEM],
         out_specs=(VMEM, VMEM),
@@ -663,24 +720,25 @@
     args = (me, pivot_owner, pivot_offset, locations, amp, nugget, covariates)
 
     column = lax.all_to_all(prep(*args, sizes[0] * sizes[3]), ("z", "c"), 0, 0, tiled=True)
-    high, middle, low, feat, base, info, match, comb, most = aux(*args)
+    high, middle, low, feat, base, info, match, comb, left, most = aux(*args)
 
     def rest(seats):
-        def run(column, comb, info, match, feat, base, high, middle, low):
+        def run(column, comb, info, match, feat, left, base, high, middle, low):
             message = seat(me, comb, column, sizes[1] * sizes[2], seats)
             mine = lax.all_to_all(message, ("x", "y"), 0, 0, tiled=True)
             other = lax.ppermute(mine, "c", swap)
-            return main(me, mine, other, info, match, feat, base, high, middle, low, devices)
+            scal, local_field = field(mine, info, match, feat, left)
+            return main(me, mine, other, info, scal, local_field, base, high, middle, low, devices)
 
         return run
 
-    operands = (column, comb, info, match, feat, base, high, middle, low)
+    operands = (column, comb, info, match, feat, left, base, high, middle, low)
     if FEW:
         factor, resid, sums = lax.cond(most[0] <= FEW, rest(FEW), rest(BLOCK), *operands)
     else:
         factor, resid, sums = rest(BLOCK)(*operands)
     all_sums = lax.all_to_all(sums[:, None, :], AXES, 0, 0, tiled=True)
-    weights, mean_residual = last(all_sums, resid, blocks)
+    weights, mean_residual = last(all_sums, resid, blocks, locations.shape[1] * devices)
     return (factor, weights.reshape(-1), mean_residual.reshape(-1))
 
 

time: 94.2 us -> 94.3 us (level)
  waiting for transfers between devices: 7.43 us -> 1.64 us
  local copies, waits for them, and re-layouts: 0.03 us -> 3.51 us
  blocking collectives: 36.1 us -> 38 us
    pallas_call x1, Pallas kernels: 30.3 us -> 24.8 us  [main(): pl.pallas_call(main_kernel, out_shape=(shape((rows, pivots)), shape((rows...]
    pallas_call x1 -> x2, Pallas kernels: 0.81 us -> 5.64 us  [the longest x1 4.83 us: field(): pl.pallas_call(field_kernel, out_shape=(shape((SUB, pivots)), shape((rows...]
    all_to_all x1, waiting for transfers between devices: 5.9 us -> 1.64 us  [local(): lax.all_to_all(prep(*args, sizes[0] * sizes[3]), ('z', 'c'), 0, 0, tiled=...]
    unnamed x12, local copies, waits for them, and re-layouts: 0.03 us -> 3.51 us
    all_to_all x1, blocking collectives: 18.2 us -> 20.4 us  [local(): all_sums = lax.all_to_all(sums[:, None, :], AXES, 0, 0, tiled=True)]
    ppermute x1, waiting for transfers between devices: 1.54 us -> 0.01 us  [run(): other = lax.ppermute(mine, 'c', swap)]
  transfers between devices with their start and end apart: 2 -> 2, of which waited for: 2 -> 1; matrix products, arithmetic and copies ran while one was open for 0% -> 0% of each run, Pallas kernels for 4% -> 10%
where the time goes in v3:
time: 94.3 us; the launch traced here: 93.8 us
  blocking collectives  38 us (40%)
  Pallas kernels  37.8 us (40%)
  starting transfers between devices  11.5 us (12%)
  local copies, waits for them, and re-layouts  3.51 us (4%)
  waiting for transfers between devices  1.64 us (2%)
  between operations  1.34 us (1%)
    pallas_call x1, Pallas kernels, main(): pl.pallas_call(main_kernel, out_shape=(shape((rows, pivots)), shape((rows...  24.8 us
    all_to_all x1, blocking collectives, local(): all_sums = lax.all_to_all(sums[:, None, :], AXES, 0, 0, tiled=True)  20.4 us
    all_to_all x1, blocking collectives, run(): mine = lax.all_to_all(message, ('x', 'y'), 0, 0, tiled=True)  17.6 us
    all_to_all x1, starting transfers between devices, local(): lax.all_to_all(prep(*args, sizes[0] * sizes[3]), ('z', 'c'), 0, 0, tiled=...  10.1 us
    pallas_call x1, Pallas kernels, field(): pl.pallas_call(field_kernel, out_shape=(shape((SUB, pivots)), shape((rows...  4.83 us
    pallas_call x1, Pallas kernels, aux(): pl.pallas_call(aux_kernel, out_shape=(shape((rows, width), jnp.bfloat16),...  4.5 us
    unnamed x12, local copies, waits for them, and re-layouts  3.51 us
    pallas_call x1, Pallas kernels, prep(): pl.pallas_call(prep_kernel, out_shape=shape((copies, 2 * slots + SUB, BLO...  2.65 us
  transfers between devices with their start and end apart: 2, of which 1 were waited for; matrix products, arithmetic and copies ran while one was open for 0% of the time, Pallas kernels for 10%

profile of v3, /device:TPU:1, one launch (start us, length us, event | category | flops | bytes accessed | tf_op | source)
XLA Modules:
  0.0 93.8 jit_solution(14810904975902496934)
XLA Ops:
  0.6 0.0 copy-start
  0.7 2.6 %prep.1 = f32[16,24,128]{2,1,0:T(8,128)} custom-call(s32[1]{0:T(128)} %bitcast.me_ref, s32[4,128]{1,0:T(4,128)} %owner_hbm.1, s32[4,128]{1,0:T(4,128)} %offset_hbm.1, f32[3,2048]{1,0:T(4,128)} %points_hbm.1, f32[1,2048]{1,0:T(1,128)} %bitcast.7, f32[1,2048]{1,0:T(1,128)} %bitcast.9, f32[2048,256]{1,0:T(8,128)} %cov_hbm.1), custom_call_target="tpu_custom_call" | custom-call | tf_op jit(solution)/shard_map/prep/pallas_call | solution.py:613
  3.3 10.1 %all-to-all-start.2 = ((f32[16,24,128]{2,1,0:T(8,128)}), f32[16,24,128]{2,1,0:T(8,128)S(1)}, u32[]{:S(2)}, u32[]{:S(2)}) async-start(f32[16,24,128]{2,1,0:T(8,128)} %prep.1), calls=%async_computation.2 | async-start | bytes 393216 | tf_op jit(solution)/shard_map/all_to_all | solution.py:722
  13.4 0.0 copy-done
  13.4 0.0 copy-start.1
  13.4 0.7 copy-done.1
  14.2 0.0 copy-start.2
  14.2 0.7 copy-done.2
  14.9 0.0 copy-start.3
  14.9 0.7 copy-done.3
  15.6 0.0 copy-start.4
  15.6 0.7 copy-done.4
  16.3 0.0 copy-start.5
  16.3 0.7 copy-done.5
  16.9 4.5 %aux.1 = (bf16[2048,256]{1,0:T(8,128)(2,1)S(1)}, bf16[2048,256]{1,0:T(8,128)(2,1)}, bf16[2048,256]{1,0:T(8,128)(2,1)}, f32[8,2048]{1,0:T(8,128)S(1)}, f32[16,128...) custom-call(s32[1]{0:T(128)} %bitcast.me_ref, ...), custom_call_target="tpu_custom_call" | custom-call | flops 100000000 | bytes 6291456 | tf_op jit(solution)/shard_map/aux/pallas_call | solution.py:631
  22.1 1.6 %all-to-all-done.2 = f32[16,24,128]{2,1,0:T(8,128)S(1)} async-done(((f32[16,24,128]{2,1,0:T(8,128)}), f32[16,24,128]{2,1,0:T(8,128)S(1)}, u32[]{:S(2)}, u32[]{:S(2)}) %all-to-all-start.2) | async-done | bytes 196640 | tf_op jit(solution)/shard_map/all_to_all | solution.py:722
  23.7 48.8 %conditional.1 = ((f32[2048,512]{1,0:T(8,128)}, f32[16,128]{1,0:T(8,128)S(1)}, f32[256,128]{1,0:T(8,128)S(1)})) conditional(s32[]{:T(128)} %bitcast.3, (s32[1]{0:T(128)}, f32[128,128]{1,0:T(8,128)S(1)}, f32[16,24,128]{2,1,0:T(8,128)S(1)}, f32[8,128]{1,0:T(8,128)S(1)}, s32[1,512]{1,0:T(1,128)S(1)}, /*index=5*/f32[8,2048]{1,0:T(8,128)S(1)}, ...), branch_computations={%region_0.0_spmd, %region_1.0_spmd} | conditional | flops 100000000 | bytes 21364840 | solution.py:737
  23.7 0.2 seat.3
  24.0 17.6 %all_to_all.19.mine_ref = f32[16,64,128]{2,1,0:T(8,128)S(1)} all-to-all(f32[16,64,128]{2,1,0:T(8,128)S(1)} %seat.3), channel_id=1, replica_groups=mesh['z'=8,'x'=4,'y'=4,'c'=2] {'x','y'}, dimensions={0} | all-to-all | bytes 1048576 | tf_op jit(solution)/shard_map/cond/branch_1_fun/all_to_all | solution.py:728
  41.6 1.4 %collective-permute-start.1 = (f32[16,64,128]{2,1,0:T(8,128)S(1)}, f32[16,64,128]{2,1,0:T(8,128)S(1)}, u32[]{:S(2)}, u32[]{:S(2)}) collective-permute-start(f32[16,64,128]{2,1,0:T(8,128)S(1)} %all_to_all.19.mine_ref), channel_id=1, source_target_pairs={{0,1},{1,0},{2,3},{3,2},{4,5},{5,4},{6,7},{7,6},{8,9},{9,8},{10,11... | collective-permute-start | bytes 1572872 | tf_op jit(solution)/shard_map/cond/branch_1_fun/ppermute | solution.py:729
  43.0 4.8 %field.3 = (f32[8,512]{1,0:T(8,128)S(1)}, f32[2048,512]{1,0:T(8,128)S(1)}) custom-call(f32[16,64,128]{2,1,0:T(8,128)S(1)} %all_to_all.19.mine_ref, f32[8,128]{1,0:T(8,128)S(1)} %get-tuple-element.60.info_ref, s32[1,512]{1,0:T(1,128)S(1)} %get-tuple-element.61.match_ref, f32[8,2048]{1,0:T(8,128)S(1)} %get-tuple-element.62.feat_ref, ...), custom_call_target="tpu_custom_call" | custom-call | flops 100000000 | bytes 6291456 | tf_op jit(solution)/shard_map/cond/branch_1_fun/field/pallas_call | solution.py:666
  47.8 0.0 collective-permute-done.1.other_ref
  47.8 24.8 %factor_rows.3 = (f32[2048,512]{1,0:T(8,128)}, f32[16,128]{1,0:T(8,128)S(1)}, f32[256,128]{1,0:T(8,128)S(1)}) custom-call(s32[1]{0:T(128)} %get-tuple-element.57.me_ref, f32[16,64,128]{2,1,0:T(8,128)S(1)} %all_to_all.19.mine_ref, f32[16,64,128]{2,1,0:T(8,128)S(1)} %collective-permute-done.1.other_ref, f32[8,128]{1,0:T(8,128)S(1)} %get-tuple-element.60.info_ref, ...), custom_call_target="tpu_custom_call" | custom-call | tf_op jit(solution)/shard_map/cond/branch_1_fun/factor_rows/pallas_call | solution.py:682
  72.6 20.4 %all_to_all.20.sums_ref = f32[256,1,128]{2,1,0:T(1,128)S(1)} all-to-all(f32[256,1,128]{2,1,0:T(1,128)S(1)} %bitcast.11), channel_id=1, replica_groups=mesh['z'=8,'x'=4,'y'=4,'c'=2] {'z','x','y','c'}, dimensions={0} | all-to-all | bytes 262144 | tf_op jit(solution)/shard_map/all_to_all | solution.py:740
  93.0 0.8 last.1
Async XLA Ops:
  0.6 12.8 %copy-start = (f32[2048,256]{1,0:T(8,128)S(1)}, f32[2048,256]{1,0:T(8,128)}, u32[]{:S(2)}) copy-start(f32[2048,256]{1,0:T(8,128)} %cov_hbm.1) | copy-start | bytes 6291460
  3.3 20.4 %all-to-all-start.2 = ((f32[16,24,128]{2,1,0:T(8,128)}), f32[16,24,128]{2,1,0:T(8,128)S(1)}, u32[]{:S(2)}, u32[]{:S(2)}) async-start(f32[16,24,128]{2,1,0:T(8,128)} %prep.1), calls=%async_computation.2 | async-start | bytes 393216 | tf_op jit(solution)/shard_map/all_to_all | solution.py:722
  13.4 0.8 copy-start.1
  14.2 0.7 copy-start.2
  14.9 0.7 copy-start.3
  15.6 0.7 copy-start.4
  16.3 0.7 copy-start.5
  41.6 6.3 %collective-permute-start.1 = (f32[16,64,128]{2,1,0:T(8,128)S(1)}, f32[16,64,128]{2,1,0:T(8,128)S(1)}, u32[]{:S(2)}, u32[]{:S(2)}) collective-permute-start(f32[16,64,128]{2,1,0:T(8,128)S(1)} %all_to_all.19.mine_ref), channel_id=1, source_target_pairs={{0,1},{1,0},{2,3},{3,2},{4,5},{5,4},{6,7},{7,6},{8,9},{9,8},{10,11... | collective-permute-start | bytes 1572872 | tf_op jit(solution)/shard_map/cond/branch_1_fun/ppermute | solution.py:729

commit v4 on v3

--- a/solution.py
+++ b/solution.py
@@ -237,12 +237,12 @@
 
 def aux_kernel(
     me_ref,
-    owner_ref,
-    offset_ref,
-    points_ref,
-    amp_ref,
-    noise_ref,
-    cov_ref,
+    owner_hbm,
+    offset_hbm,
+    points_hbm,
+    amp_hbm,
+    noise_hbm,
+    cov_hbm,
     high_ref,
     middle_ref,
     low_ref,
@@ -253,9 +253,29 @@
     comb_ref,
     left_ref,
     most_ref,
+    owner_ref,
+    offset_ref,
+    points_ref,
+    amp_ref,
+    noise_ref,
+    cov_ref,
+    load_sem,
 ):
+    pairs = (
+        (owner_hbm, owner_ref),
+        (offset_hbm, offset_ref),
+        (points_hbm, points_ref),
+        (amp_hbm, amp_ref),
+        (noise_hbm, noise_ref),
+        (cov_hbm, cov_ref),
+    )
+    loads = [pltpu.make_async_copy(*pair, load_sem.at[i]) for i, pair in enumerate(pairs)]
+    for load in loads:
+        load.start()
     me = me_ref[0]
     blocks, width = owner_ref.shape
+    for load in loads[:2]:
+        load.wait()
     local_rows, cov_width = cov_ref.shape
     half = cov_width // 2
     owner = owner_ref[...]
@@ -296,6 +316,8 @@
     candidate_hit = (ids == candidate).astype(jnp.float32).astype(jnp.bfloat16)
     comb_ref[...] = product(seat_hit, candidate_hit, ((1,), (1,)))
 
+    for load in loads[2:]:
+        load.wait()
     feat_ref[:3, :] = points_ref[...]
     feat_ref[3:4, :] = amp_ref[...]
     feat_ref[4:5, :] = noise_ref[...]
@@ -606,6 +628,7 @@
 SMEM = pl.BlockSpec(memory_space=pltpu.SMEM)
 ANY = pl.BlockSpec(memory_space=pl.ANY)
 PARAMS = pltpu.CompilerParams(vmem_limit_bytes=40 << 20)
+AUX_PARAMS = pltpu.CompilerParams(vmem_limit_bytes=55 << 20)
 
 
 def prep(me, owner, offset, points, amp, noise, cov, copies):
@@ -642,9 +665,11 @@
             shape((rows, BLOCK), jnp.bfloat16),
             shape((1,), jnp.int32),
         ),
-        in_specs=[SMEM] + [VMEM] * 6,
+        in_specs=[SMEM] + [ANY] * 6,
         out_specs=(VMEM,) * 9 + (SMEM,),
-        compiler_params=PARAMS,
+        scratch_shapes=[pltpu.VMEM(value.shape, value.dtype) for value in (owner, offset, points, amp, noise, cov)]
+        + [pltpu.SemaphoreType.DMA((6,))],
+        compiler_params=AUX_PARAMS,
         cost_estimate=pl.CostEstimate(flops=10**8, bytes_accessed=6 << 20, transcendentals=0),
         name="aux",
     )(me, owner, offset, points, amp, noise, cov)

time: 94.3 us -> 91.6 us (0.971)
  local copies, waits for them, and re-layouts: 3.51 us -> 0 us
  waiting for transfers between devices: 1.64 us -> 4.61 us
  blocking collectives: 38 us -> 35.4 us
    unnamed x12 -> x0, local copies, waits for them, and re-layouts: 3.51 us -> none
    all_to_all x1, waiting for transfers between devices: 1.64 us -> 4.61 us  [local(): lax.all_to_all(prep(*args, sizes[0] * sizes[3]), ('z', 'c'), 0, 0, tiled=...]
    all_to_all x1, blocking collectives: 20.4 us -> 17.8 us  [local(): all_sums = lax.all_to_all(sums[:, None, :], AXES, 0, 0, tiled=True)]
  transfers between devices with their start and end apart: 2 -> 2, of which waited for: 1 -> 1; matrix products, arithmetic and copies ran while one was open for 0% -> 0% of each run, Pallas kernels for 10% -> 11%
where the time goes in v4:
time: 91.6 us; the launch traced here: 91.1 us
  Pallas kernels  38.5 us (42%)
  blocking collectives  35.4 us (39%)
  starting transfers between devices  11.3 us (12%)
  waiting for transfers between devices  4.61 us (5%)
  between operations  1.31 us (1%)
    pallas_call x1, Pallas kernels, main(): pl.pallas_call(main_kernel, out_shape=(shape((rows, pivots)), shape((rows...  24.9 us
    all_to_all x1, blocking collectives, local(): all_sums = lax.all_to_all(sums[:, None, :], AXES, 0, 0, tiled=True)  17.8 us
    all_to_all x1, blocking collectives, run(): mine = lax.all_to_all(message, ('x', 'y'), 0, 0, tiled=True)  17.6 us
    all_to_all x1, starting transfers between devices, local(): lax.all_to_all(prep(*args, sizes[0] * sizes[3]), ('z', 'c'), 0, 0, tiled=...  9.89 us
    pallas_call x1, Pallas kernels, aux(): pl.pallas_call(aux_kernel, out_shape=(shape((rows, width), jnp.bfloat16),...  5.06 us
    pallas_call x1, Pallas kernels, field(): pl.pallas_call(field_kernel, out_shape=(shape((SUB, pivots)), shape((rows...  4.83 us
    all_to_all x1, waiting for transfers between devices, local(): lax.all_to_all(prep(*args, sizes[0] * sizes[3]), ('z', 'c'), 0, 0, tiled=...  4.61 us
    pallas_call x1, Pallas kernels, prep(): pl.pallas_call(prep_kernel, out_shape=shape((copies, 2 * slots + SUB, BLO...  2.61 us
  transfers between devices with their start and end apart: 2, of which 1 were waited for; matrix products, arithmetic and copies ran while one was open for 0% of the time, Pallas kernels for 11%

profile of v4, /device:TPU:1, one launch (start us, length us, event | category | flops | bytes accessed | tf_op | source)
XLA Modules:
  0.0 91.1 jit_solution(1349405856295324729)
XLA Ops:
  0.6 2.6 %prep.1 = f32[16,24,128]{2,1,0:T(8,128)} custom-call(s32[1]{0:T(128)} %bitcast.me_ref, s32[4,128]{1,0:T(4,128)} %owner_hbm.3, s32[4,128]{1,0:T(4,128)} %offset_hbm.3, f32[3,2048]{1,0:T(4,128)} %points_hbm.3, f32[1,2048]{1,0:T(1,128)} %bitcast.8, f32[1,2048]{1,0:T(1,128)} %bitcast.10, f32[2048,256]{1,0:T(8,128)} %cov_hbm.3), custom_call_target="tpu_custom_call" | custom-call | tf_op jit(solution)/shard_map/prep/pallas_call | solution.py:636
  3.3 9.9 %all-to-all-start.2 = ((f32[16,24,128]{2,1,0:T(8,128)}), f32[16,24,128]{2,1,0:T(8,128)S(1)}, u32[]{:S(2)}, u32[]{:S(2)}) async-start(f32[16,24,128]{2,1,0:T(8,128)} %prep.1), calls=%async_computation.2 | async-start | bytes 393216 | tf_op jit(solution)/shard_map/all_to_all | solution.py:747
  13.1 5.1 %aux.1 = (bf16[2048,256]{1,0:T(8,128)(2,1)S(1)}, bf16[2048,256]{1,0:T(8,128)(2,1)S(1)}, bf16[2048,256]{1,0:T(8,128)(2,1)S(1)}, f32[8,2048]{1,0:T(8,128)S(1)}, f3...) custom-call(s32[1]{0:T(128)} %bitcast.me_ref, ...), custom_call_target="tpu_custom_call" | custom-call | flops 100000000 | bytes 6291456 | tf_op jit(solution)/shard_map/aux/pallas_call | solution.py:654
  18.9 4.6 %all-to-all-done.2 = f32[16,24,128]{2,1,0:T(8,128)S(1)} async-done(((f32[16,24,128]{2,1,0:T(8,128)}), f32[16,24,128]{2,1,0:T(8,128)S(1)}, u32[]{:S(2)}, u32[]{:S(2)}) %all-to-all-start.2) | async-done | bytes 196640 | tf_op jit(solution)/shard_map/all_to_all | solution.py:747
  23.5 49.0 %conditional.1 = ((f32[2048,512]{1,0:T(8,128)}, f32[16,128]{1,0:T(8,128)S(1)}, f32[256,128]{1,0:T(8,128)S(1)})) conditional(s32[]{:T(128)} %bitcast.3, (s32[1]{0:T(128)}, f32[128,128]{1,0:T(8,128)S(1)}, f32[16,24,128]{2,1,0:T(8,128)S(1)}, f32[8,128]{1,0:T(8,128)S(1)}, s32[1,512]{1,0:T(1,128)S(1)}, /*index=5*/f32[8,2048]{1,0:T(8,128)S(1)}, ...), branch_computations={%region_0.0_spmd, %region_1.0_spmd} | conditional | flops 100000000 | bytes 12976176 | solution.py:762
  23.5 0.2 seat.3
  23.7 17.6 %all_to_all.19.mine_ref = f32[16,64,128]{2,1,0:T(8,128)S(1)} all-to-all(f32[16,64,128]{2,1,0:T(8,128)S(1)} %seat.3), channel_id=1, replica_groups=mesh['z'=8,'x'=4,'y'=4,'c'=2] {'x','y'}, dimensions={0} | all-to-all | bytes 1048576 | tf_op jit(solution)/shard_map/cond/branch_1_fun/all_to_all | solution.py:753
  41.3 1.4 %collective-permute-start.1 = (f32[16,64,128]{2,1,0:T(8,128)S(1)}, f32[16,64,128]{2,1,0:T(8,128)S(1)}, u32[]{:S(2)}, u32[]{:S(2)}) collective-permute-start(f32[16,64,128]{2,1,0:T(8,128)S(1)} %all_to_all.19.mine_ref), channel_id=1, source_target_pairs={{0,1},{1,0},{2,3},{3,2},{4,5},{5,4},{6,7},{7,6},{8,9},{9,8},{10,11... | collective-permute-start | bytes 1572872 | tf_op jit(solution)/shard_map/cond/branch_1_fun/ppermute | solution.py:754
  42.7 4.8 %field.3 = (f32[8,512]{1,0:T(8,128)S(1)}, f32[2048,512]{1,0:T(8,128)S(1)}) custom-call(f32[16,64,128]{2,1,0:T(8,128)S(1)} %all_to_all.19.mine_ref, f32[8,128]{1,0:T(8,128)S(1)} %get-tuple-element.60.info_ref, s32[1,512]{1,0:T(1,128)S(1)} %get-tuple-element.61.match_ref, f32[8,2048]{1,0:T(8,128)S(1)} %get-tuple-element.62.feat_ref, ...), custom_call_target="tpu_custom_call" | custom-call | flops 100000000 | bytes 6291456 | tf_op jit(solution)/shard_map/cond/branch_1_fun/field/pallas_call | solution.py:691
  47.5 0.0 collective-permute-done.1.other_ref
  47.6 24.9 %factor_rows.3 = (f32[2048,512]{1,0:T(8,128)}, f32[16,128]{1,0:T(8,128)S(1)}, f32[256,128]{1,0:T(8,128)S(1)}) custom-call(s32[1]{0:T(128)} %get-tuple-element.57.me_ref, f32[16,64,128]{2,1,0:T(8,128)S(1)} %all_to_all.19.mine_ref, f32[16,64,128]{2,1,0:T(8,128)S(1)} %collective-permute-done.1.other_ref, f32[8,128]{1,0:T(8,128)S(1)} %get-tuple-element.60.info_ref, ...), custom_call_target="tpu_custom_call" | custom-call | tf_op jit(solution)/shard_map/cond/branch_1_fun/factor_rows/pallas_call | solution.py:707
  72.5 17.8 %all_to_all.20.sums_ref = f32[256,1,128]{2,1,0:T(1,128)S(1)} all-to-all(f32[256,1,128]{2,1,0:T(1,128)S(1)} %bitcast.7), channel_id=1, replica_groups=mesh['z'=8,'x'=4,'y'=4,'c'=2] {'z','x','y','c'}, dimensions={0} | all-to-all | bytes 262144 | tf_op jit(solution)/shard_map/all_to_all | solution.py:765
  90.3 0.8 last.1
Async XLA Ops:
  3.3 20.2 %all-to-all-start.2 = ((f32[16,24,128]{2,1,0:T(8,128)}), f32[16,24,128]{2,1,0:T(8,128)S(1)}, u32[]{:S(2)}, u32[]{:S(2)}) async-start(f32[16,24,128]{2,1,0:T(8,128)} %prep.1), calls=%async_computation.2 | async-start | bytes 393216 | tf_op jit(solution)/shard_map/all_to_all | solution.py:747
  41.3 6.3 %collective-permute-start.1 = (f32[16,64,128]{2,1,0:T(8,128)S(1)}, f32[16,64,128]{2,1,0:T(8,128)S(1)}, u32[]{:S(2)}, u32[]{:S(2)}) collective-permute-start(f32[16,64,128]{2,1,0:T(8,128)S(1)} %all_to_all.19.mine_ref), channel_id=1, source_target_pairs={{0,1},{1,0},{2,3},{3,2},{4,5},{5,4},{6,7},{7,6},{8,9},{9,8},{10,11... | collective-permute-start | bytes 1572872 | tf_op jit(solution)/shard_map/cond/branch_1_fun/ppermute | solution.py:754

commit v5 on v4

--- a/solution.py
+++ b/solution.py
@@ -27,9 +27,9 @@
     )
 
 
-def panel_inverse(low, high):
+def panel_rows(low, high, near, top, bottom, near_rows):
     sub = lax.broadcasted_iota(jnp.int32, (SUB, BLOCK), 0)
-    low, high = list(low), list(high)
+    low, high, near, near_rows = list(low), list(high), [list(one) for one in near], list(near_rows)
     root_low = jnp.zeros((SUB, BLOCK), jnp.float32)
     root_high = root_low
 
@@ -44,36 +44,28 @@
         if k + 1 < PANEL:
             side = entry(k, k + 1)
             pivot = entry(k + 1, k + 1) - (side * side) * inverse
+        take_near = [one[k] * inverse for one in near]
         if k < SUB:
             take_low = jnp.where(sub > k, low[k], 0.0) * inverse
             take_high = high[k] * inverse
-            across = high[k]
             root_low = jnp.where(sub == k, root, root_low)
-            for j in range(PANEL):
-                if j < SUB and j != k:
-                    line = low[j][k : k + 1, :]
-                    low[j] = low[j] - take_low * line
-                    high[j] = high[j] - take_high * line
-                elif j >= SUB:
-                    high[j] = high[j] - take_high * across[j - SUB : j - SUB + 1, :]
-            low[k] = jnp.where(sub == k, 1.0, -take_low)
-            high[k] = -take_high
+            line = top[k : k + 1, :]
         else:
-            s = k - SUB
-            take_high = jnp.where(sub > s, high[k], 0.0) * inverse
-            root_high = jnp.where(sub == s, root, root_high)
-            for j in range(PANEL):
-                if j != k:
-                    high[j] = high[j] - take_high * high[j][s : s + 1, :]
-            high[k] = jnp.where(sub == s, 1.0, -take_high)
-    return [low[j] * root_low for j in range(SUB)], [high[j] * root_high for j in range(PANEL)]
-
-
-def tree_sum(terms):
-    while len(terms) > 1:
-        pairs = [terms[i] + terms[i + 1] for i in range(0, len(terms) - 1, 2)]
-        terms = pairs + terms[2 * len(pairs) :]
-    return terms[0]
+            take_high = jnp.where(sub > k - SUB, high[k], 0.0) * inverse
+            root_high = jnp.where(sub == k - SUB, root, root_high)
+            line = bottom[k - SUB : k - SUB + 1, :]
+        for j in range(k + 1, PANEL):
+            across = entry(k, j)
+            if j < SUB:
+                low[j] = low[j] - take_low * across
+            high[j] = high[j] - take_high * across
+            for one, take in zip(near, take_near):
+                one[j] = one[j] - take * across
+        if k < SUB:
+            top = top - take_low * line
+        bottom = bottom - take_high * line
+        near_rows = [row - take * line for row, take in zip(near_rows, take_near)]
+    return top * root_low, bottom * root_high, near_rows
 
 
 def block_inverse(rows):
@@ -92,36 +84,25 @@
         near, far = rest[:2], rest[2:]
         low = [splat(rows[at], j) for j in range(SUB)]
         high = [splat(rows[at + 1], j) for j in range(PANEL)]
-        coef = {r: [splat(rows[r], j) for j in range(PANEL)] for r in near}
-        inv_low, inv_high = panel_inverse(low, high)
+        next_columns = [[splat(rows[r], j) for j in range(PANEL)] for r in near]
         in_panel = (lane >= first) & (lane < first + PANEL)
         top = jnp.where(in_panel, jnp.where(lane - first == sub, 1.0, 0.0), rows[at])
         bottom = jnp.where(in_panel, jnp.where(lane - first - SUB == sub, 1.0, 0.0), rows[at + 1])
-        entries = [top[j : j + 1, :] for j in range(SUB)] + [bottom[j : j + 1, :] for j in range(SUB)]
-        new_low = tree_sum([inv_low[j] * entries[j] for j in range(SUB)])
-        new_high = tree_sum([inv_high[j] * entries[j] for j in range(PANEL)])
+        next_rows = [jnp.where(in_panel, 0.0, rows[r]) for r in near]
+        new_low, new_high, next_rows = panel_rows(low, high, next_columns, top, bottom, next_rows)
         out[at] = jnp.where(lane <= first + sub, new_low, 0.0)
         out[at + 1] = jnp.where(lane <= first + SUB + sub, new_high, 0.0)
-        if len(near):
-            weights = []
-            for j in range(PANEL):
-                term = inv_high[j] * new_high
-                if j < SUB:
-                    term = term + inv_low[j] * new_low
-                weights.append(jnp.sum(term, axis=0, keepdims=True))
-            for r in near:
-                piece = jnp.where(in_panel, 0.0, rows[r])
-                for j in range(PANEL):
-                    piece = piece - coef[r][j] * weights[j]
-                rows[r] = piece
+        for r, row in zip(near, next_rows):
+            rows[r] = row
         if len(far):
-            spread = []
-            for part in parts_of(jnp.concatenate(weights, axis=0)):
-                above = [jnp.zeros((first, BLOCK), jnp.bfloat16)] if first else []
-                below = [jnp.zeros((BLOCK - first - PANEL, BLOCK), jnp.bfloat16)]
-                spread.append(jnp.concatenate(above + [part] + below, axis=0))
-            far_rows = parts_of(jnp.concatenate([rows[r] for r in far], axis=0))
-            change = dot_parts(far_rows, spread, ((1,), (0,)))
+            new_rows = jnp.concatenate([new_low, new_high], axis=0)
+            filler = jnp.zeros((BLOCK - PANEL, BLOCK), jnp.float32)
+            flipped = jnp.concatenate([new_rows, filler], axis=0).T
+            far_parts = parts_of(flipped[SUB * far[0] : SUB * (far[-1] + 1), :])
+            spread = [
+                jnp.concatenate([part, filler.astype(jnp.bfloat16)], axis=0) for part in parts_of(new_rows)
+            ]
+            change = dot_parts(far_parts, spread, ((1,), (0,)))
             for i, r in enumerate(far):
                 rows[r] = jnp.where(in_panel, 0.0, rows[r]) - change[SUB * i : SUB * (i + 1)]
     return out

time: 91.6 us -> 92.2 us (level)
  no operation moved by 1% of the time
where the time goes in v5:
time: 92.2 us; the launch traced here: 91.8 us
  Pallas kernels  39 us (42%)
  blocking collectives  35.4 us (38%)
  starting transfers between devices  11.4 us (12%)
  waiting for transfers between devices  4.61 us (5%)
  between operations  1.31 us (1%)
    pallas_call x1, Pallas kernels, main(): pl.pallas_call(main_kernel, out_shape=(shape((rows, pivots)), shape((rows...  25.4 us
    all_to_all x1, blocking collectives, local(): all_sums = lax.all_to_all(sums[:, None, :], AXES, 0, 0, tiled=True)  17.8 us
    all_to_all x1, blocking collectives, run(): mine = lax.all_to_all(message, ('x', 'y'), 0, 0, tiled=True)  17.6 us
    all_to_all x1, starting transfers between devices, local(): lax.all_to_all(prep(*args, sizes[0] * sizes[3]), ('z', 'c'), 0, 0, tiled=...  9.98 us
    pallas_call x1, Pallas kernels, aux(): pl.pallas_call(aux_kernel, out_shape=(shape((rows, width), jnp.bfloat16),...  5.06 us
    pallas_call x1, Pallas kernels, field(): pl.pallas_call(field_kernel, out_shape=(shape((SUB, pivots)), shape((rows...  4.83 us
    all_to_all x1, waiting for transfers between devices, local(): lax.all_to_all(prep(*args, sizes[0] * sizes[3]), ('z', 'c'), 0, 0, tiled=...  4.61 us
    pallas_call x1, Pallas kernels, prep(): pl.pallas_call(prep_kernel, out_shape=shape((copies, 2 * slots + SUB, BLO...  2.62 us
  transfers between devices with their start and end apart: 2, of which 1 were waited for; matrix products, arithmetic and copies ran while one was open for 0% of the time, Pallas kernels for 11%

profile of v5, /device:TPU:1, one launch (start us, length us, event | category | flops | bytes accessed | tf_op | source)
XLA Modules:
  0.0 91.8 jit_solution(12122549725945072950)
XLA Ops:
  0.6 2.6 %prep.1 = f32[16,24,128]{2,1,0:T(8,128)} custom-call(s32[1]{0:T(128)} %bitcast.me_ref, s32[4,128]{1,0:T(4,128)} %owner_hbm.3, s32[4,128]{1,0:T(4,128)} %offset_hbm.3, f32[3,2048]{1,0:T(4,128)} %points_hbm.3, f32[1,2048]{1,0:T(1,128)} %bitcast.8, f32[1,2048]{1,0:T(1,128)} %bitcast.10, f32[2048,256]{1,0:T(8,128)} %cov_hbm.3), custom_call_target="tpu_custom_call" | custom-call | tf_op jit(solution)/shard_map/prep/pallas_call | solution.py:617
  3.3 10.0 %all-to-all-start.2 = ((f32[16,24,128]{2,1,0:T(8,128)}), f32[16,24,128]{2,1,0:T(8,128)S(1)}, u32[]{:S(2)}, u32[]{:S(2)}) async-start(f32[16,24,128]{2,1,0:T(8,128)} %prep.1), calls=%async_computation.2 | async-start | bytes 393216 | tf_op jit(solution)/shard_map/all_to_all | solution.py:728
  13.2 5.1 %aux.1 = (bf16[2048,256]{1,0:T(8,128)(2,1)S(1)}, bf16[2048,256]{1,0:T(8,128)(2,1)S(1)}, bf16[2048,256]{1,0:T(8,128)(2,1)S(1)}, f32[8,2048]{1,0:T(8,128)S(1)}, f3...) custom-call(s32[1]{0:T(128)} %bitcast.me_ref, ...), custom_call_target="tpu_custom_call" | custom-call | flops 100000000 | bytes 6291456 | tf_op jit(solution)/shard_map/aux/pallas_call | solution.py:635
  19.0 4.6 %all-to-all-done.2 = f32[16,24,128]{2,1,0:T(8,128)S(1)} async-done(((f32[16,24,128]{2,1,0:T(8,128)}), f32[16,24,128]{2,1,0:T(8,128)S(1)}, u32[]{:S(2)}, u32[]{:S(2)}) %all-to-all-start.2) | async-done | bytes 196640 | tf_op jit(solution)/shard_map/all_to_all | solution.py:728
  23.6 49.5 %conditional.1 = ((f32[2048,512]{1,0:T(8,128)}, f32[16,128]{1,0:T(8,128)S(1)}, f32[256,128]{1,0:T(8,128)S(1)})) conditional(s32[]{:T(128)} %bitcast.3, (s32[1]{0:T(128)}, f32[128,128]{1,0:T(8,128)S(1)}, f32[16,24,128]{2,1,0:T(8,128)S(1)}, f32[8,128]{1,0:T(8,128)S(1)}, s32[1,512]{1,0:T(1,128)S(1)}, /*index=5*/f32[8,2048]{1,0:T(8,128)S(1)}, ...), branch_computations={%region_0.0_spmd, %region_1.0_spmd} | conditional | flops 100000000 | bytes 12976176 | solution.py:743
  23.6 0.2 seat.3
  23.8 17.6 %all_to_all.19.mine_ref = f32[16,64,128]{2,1,0:T(8,128)S(1)} all-to-all(f32[16,64,128]{2,1,0:T(8,128)S(1)} %seat.3), channel_id=1, replica_groups=mesh['z'=8,'x'=4,'y'=4,'c'=2] {'x','y'}, dimensions={0} | all-to-all | bytes 1048576 | tf_op jit(solution)/shard_map/cond/branch_1_fun/all_to_all | solution.py:734
  41.4 1.4 %collective-permute-start.1 = (f32[16,64,128]{2,1,0:T(8,128)S(1)}, f32[16,64,128]{2,1,0:T(8,128)S(1)}, u32[]{:S(2)}, u32[]{:S(2)}) collective-permute-start(f32[16,64,128]{2,1,0:T(8,128)S(1)} %all_to_all.19.mine_ref), channel_id=1, source_target_pairs={{0,1},{1,0},{2,3},{3,2},{4,5},{5,4},{6,7},{7,6},{8,9},{9,8},{10,11... | collective-permute-start | bytes 1572872 | tf_op jit(solution)/shard_map/cond/branch_1_fun/ppermute | solution.py:735
  42.8 4.8 %field.3 = (f32[8,512]{1,0:T(8,128)S(1)}, f32[2048,512]{1,0:T(8,128)S(1)}) custom-call(f32[16,64,128]{2,1,0:T(8,128)S(1)} %all_to_all.19.mine_ref, f32[8,128]{1,0:T(8,128)S(1)} %get-tuple-element.60.info_ref, s32[1,512]{1,0:T(1,128)S(1)} %get-tuple-element.61.match_ref, f32[8,2048]{1,0:T(8,128)S(1)} %get-tuple-element.62.feat_ref, ...), custom_call_target="tpu_custom_call" | custom-call | flops 100000000 | bytes 6291456 | tf_op jit(solution)/shard_map/cond/branch_1_fun/field/pallas_call | solution.py:672
  47.6 0.0 collective-permute-done.1.other_ref
  47.7 25.4 %factor_rows.3 = (f32[2048,512]{1,0:T(8,128)}, f32[16,128]{1,0:T(8,128)S(1)}, f32[256,128]{1,0:T(8,128)S(1)}) custom-call(s32[1]{0:T(128)} %get-tuple-element.57.me_ref, f32[16,64,128]{2,1,0:T(8,128)S(1)} %all_to_all.19.mine_ref, f32[16,64,128]{2,1,0:T(8,128)S(1)} %collective-permute-done.1.other_ref, f32[8,128]{1,0:T(8,128)S(1)} %get-tuple-element.60.info_ref, ...), custom_call_target="tpu_custom_call" | custom-call | tf_op jit(solution)/shard_map/cond/branch_1_fun/factor_rows/pallas_call | solution.py:688
  73.1 17.8 %all_to_all.20.sums_ref = f32[256,1,128]{2,1,0:T(1,128)S(1)} all-to-all(f32[256,1,128]{2,1,0:T(1,128)S(1)} %bitcast.7), channel_id=1, replica_groups=mesh['z'=8,'x'=4,'y'=4,'c'=2] {'z','x','y','c'}, dimensions={0} | all-to-all | bytes 262144 | tf_op jit(solution)/shard_map/all_to_all | solution.py:746
  91.0 0.8 last.1
Async XLA Ops:
  3.3 20.3 %all-to-all-start.2 = ((f32[16,24,128]{2,1,0:T(8,128)}), f32[16,24,128]{2,1,0:T(8,128)S(1)}, u32[]{:S(2)}, u32[]{:S(2)}) async-start(f32[16,24,128]{2,1,0:T(8,128)} %prep.1), calls=%async_computation.2 | async-start | bytes 393216 | tf_op jit(solution)/shard_map/all_to_all | solution.py:728
  41.4 6.3 %collective-permute-start.1 = (f32[16,64,128]{2,1,0:T(8,128)S(1)}, f32[16,64,128]{2,1,0:T(8,128)S(1)}, u32[]{:S(2)}, u32[]{:S(2)}) collective-permute-start(f32[16,64,128]{2,1,0:T(8,128)S(1)} %all_to_all.19.mine_ref), channel_id=1, source_target_pairs={{0,1},{1,0},{2,3},{3,2},{4,5},{5,4},{6,7},{7,6},{8,9},{9,8},{10,11... | collective-permute-start | bytes 1572872 | tf_op jit(solution)/shard_map/cond/branch_1_fun/ppermute | solution.py:735

commit v6 on v5

--- a/solution.py
+++ b/solution.py
@@ -372,7 +372,8 @@
             piece = pltpu.roll(mine_ref[q * packed + t, seats:, :], t * stride, 1)
             line = jnp.where(lane // stride == t, piece, line)
         lines.append(line)
-    line_parts = parts_of(jnp.concatenate(lines, axis=1))
+    line_parts = [part.astype(jnp.float32) for part in parts_of(jnp.concatenate(lines, axis=1))]
+    line_parts = jnp.concatenate(line_parts + [jnp.zeros_like(line_parts[0])], axis=0).astype(jnp.bfloat16)
     info_t = info_ref[...].T
     for b in range(blocks):
         here = pl.ds(b * BLOCK, BLOCK)
@@ -380,11 +381,8 @@
         place = (xy * stride + seat).astype(jnp.int32)
         ids = lax.broadcasted_iota(jnp.int32, (BLOCK, planes * stride), 1)
         line_pick = (ids == place).astype(jnp.float32).astype(jnp.bfloat16)
-        scal_ref[:, here] = (
-            product(line_parts[0], line_pick, nt)
-            + product(line_parts[1], line_pick, nt)
-            + product(line_parts[2], line_pick, nt)
-        )
+        picked = product(line_parts, line_pick, nt)
+        scal_ref[:, here] = picked[:SUB] + picked[SUB : 2 * SUB] + picked[2 * SUB : 3 * SUB]
     for t in range(local_rows // BLOCK):
         at = pl.ds(t * BLOCK, BLOCK)
         col_ref[at, :] = feat_ref[:, at].T

time: 92.2 us -> 92 us (level)
  transfers between devices with their start and end apart: 2 -> 2, of which waited for: 1 -> 1; matrix products, arithmetic and copies ran while one was open for 0% -> 0% of each run, Pallas kernels for 11% -> 10%
where the time goes in v6:
time: 92 us; the launch traced here: 91.6 us
  Pallas kernels  38.6 us (42%)
  blocking collectives  35.4 us (38%)
  starting transfers between devices  11.4 us (12%)
  waiting for transfers between devices  4.61 us (5%)
  between operations  1.31 us (1%)
    pallas_call x1, Pallas kernels, main(): pl.pallas_call(main_kernel, out_shape=(shape((rows, pivots)), shape((rows...  25.5 us
    all_to_all x1, blocking collectives, local(): all_sums = lax.all_to_all(sums[:, None, :], AXES, 0, 0, tiled=True)  17.8 us
    all_to_all x1, blocking collectives, run(): mine = lax.all_to_all(message, ('x', 'y'), 0, 0, tiled=True)  17.6 us
    all_to_all x1, starting transfers between devices, local(): lax.all_to_all(prep(*args, sizes[0] * sizes[3]), ('z', 'c'), 0, 0, tiled=...  9.99 us
    pallas_call x1, Pallas kernels, aux(): pl.pallas_call(aux_kernel, out_shape=(shape((rows, width), jnp.bfloat16),...  5.06 us
    all_to_all x1, waiting for transfers between devices, local(): lax.all_to_all(prep(*args, sizes[0] * sizes[3]), ('z', 'c'), 0, 0, tiled=...  4.61 us
    pallas_call x1, Pallas kernels, field(): pl.pallas_call(field_kernel, out_shape=(shape((SUB, pivots)), shape((rows...  4.43 us
    pallas_call x1, Pallas kernels, prep(): pl.pallas_call(prep_kernel, out_shape=shape((copies, 2 * slots + SUB, BLO...  2.62 us
  transfers between devices with their start and end apart: 2, of which 1 were waited for; matrix products, arithmetic and copies ran while one was open for 0% of the time, Pallas kernels for 10%

profile of v6, /device:TPU:1, one launch (start us, length us, event | category | flops | bytes accessed | tf_op | source)
XLA Modules:
  0.0 91.6 jit_solution(16800599491757575199)
XLA Ops:
  0.6 2.6 %prep.1 = f32[16,24,128]{2,1,0:T(8,128)} custom-call(s32[1]{0:T(128)} %bitcast.me_ref, s32[4,128]{1,0:T(4,128)} %owner_hbm.3, s32[4,128]{1,0:T(4,128)} %offset_hbm.3, f32[3,2048]{1,0:T(4,128)} %points_hbm.3, f32[1,2048]{1,0:T(1,128)} %bitcast.8, f32[1,2048]{1,0:T(1,128)} %bitcast.10, f32[2048,256]{1,0:T(8,128)} %cov_hbm.3), custom_call_target="tpu_custom_call" | custom-call | tf_op jit(solution)/shard_map/prep/pallas_call | solution.py:615
  3.3 10.0 %all-to-all-start.2 = ((f32[16,24,128]{2,1,0:T(8,128)}), f32[16,24,128]{2,1,0:T(8,128)S(1)}, u32[]{:S(2)}, u32[]{:S(2)}) async-start(f32[16,24,128]{2,1,0:T(8,128)} %prep.1), calls=%async_computation.2 | async-start | bytes 393216 | tf_op jit(solution)/shard_map/all_to_all | solution.py:726
  13.3 5.1 %aux.1 = (bf16[2048,256]{1,0:T(8,128)(2,1)S(1)}, bf16[2048,256]{1,0:T(8,128)(2,1)S(1)}, bf16[2048,256]{1,0:T(8,128)(2,1)S(1)}, f32[8,2048]{1,0:T(8,128)S(1)}, f3...) custom-call(s32[1]{0:T(128)} %bitcast.me_ref, ...), custom_call_target="tpu_custom_call" | custom-call | flops 100000000 | bytes 6291456 | tf_op jit(solution)/shard_map/aux/pallas_call | solution.py:633
  19.0 4.6 %all-to-all-done.2 = f32[16,24,128]{2,1,0:T(8,128)S(1)} async-done(((f32[16,24,128]{2,1,0:T(8,128)}), f32[16,24,128]{2,1,0:T(8,128)S(1)}, u32[]{:S(2)}, u32[]{:S(2)}) %all-to-all-start.2) | async-done | bytes 196640 | tf_op jit(solution)/shard_map/all_to_all | solution.py:726
  23.6 49.4 %conditional.1 = ((f32[2048,512]{1,0:T(8,128)}, f32[16,128]{1,0:T(8,128)S(1)}, f32[256,128]{1,0:T(8,128)S(1)})) conditional(s32[]{:T(128)} %bitcast.3, (s32[1]{0:T(128)}, f32[128,128]{1,0:T(8,128)S(1)}, f32[16,24,128]{2,1,0:T(8,128)S(1)}, f32[8,128]{1,0:T(8,128)S(1)}, s32[1,512]{1,0:T(1,128)S(1)}, /*index=5*/f32[8,2048]{1,0:T(8,128)S(1)}, ...), branch_computations={%region_0.0_spmd, %region_1.0_spmd} | conditional | flops 100000000 | bytes 12976176 | solution.py:741
  23.6 0.2 seat.3
  23.8 17.6 %all_to_all.19.mine_ref = f32[16,64,128]{2,1,0:T(8,128)S(1)} all-to-all(f32[16,64,128]{2,1,0:T(8,128)S(1)} %seat.3), channel_id=1, replica_groups=mesh['z'=8,'x'=4,'y'=4,'c'=2] {'x','y'}, dimensions={0} | all-to-all | bytes 1048576 | tf_op jit(solution)/shard_map/cond/branch_1_fun/all_to_all | solution.py:732
  41.4 1.4 %collective-permute-start.1 = (f32[16,64,128]{2,1,0:T(8,128)S(1)}, f32[16,64,128]{2,1,0:T(8,128)S(1)}, u32[]{:S(2)}, u32[]{:S(2)}) collective-permute-start(f32[16,64,128]{2,1,0:T(8,128)S(1)} %all_to_all.19.mine_ref), channel_id=1, source_target_pairs={{0,1},{1,0},{2,3},{3,2},{4,5},{5,4},{6,7},{7,6},{8,9},{9,8},{10,11... | collective-permute-start | bytes 1572872 | tf_op jit(solution)/shard_map/cond/branch_1_fun/ppermute | solution.py:733
  42.8 4.4 %field.3 = (f32[8,512]{1,0:T(8,128)S(1)}, f32[2048,512]{1,0:T(8,128)S(1)}) custom-call(f32[16,64,128]{2,1,0:T(8,128)S(1)} %all_to_all.19.mine_ref, f32[8,128]{1,0:T(8,128)S(1)} %get-tuple-element.60.info_ref, s32[1,512]{1,0:T(1,128)S(1)} %get-tuple-element.61.match_ref, f32[8,2048]{1,0:T(8,128)S(1)} %get-tuple-element.62.feat_ref, ...), custom_call_target="tpu_custom_call" | custom-call | flops 100000000 | bytes 6291456 | tf_op jit(solution)/shard_map/cond/branch_1_fun/field/pallas_call | solution.py:670
  47.3 0.0 collective-permute-done.1.other_ref
  47.3 25.5 %factor_rows.3 = (f32[2048,512]{1,0:T(8,128)}, f32[16,128]{1,0:T(8,128)S(1)}, f32[256,128]{1,0:T(8,128)S(1)}) custom-call(s32[1]{0:T(128)} %get-tuple-element.57.me_ref, f32[16,64,128]{2,1,0:T(8,128)S(1)} %all_to_all.19.mine_ref, f32[16,64,128]{2,1,0:T(8,128)S(1)} %collective-permute-done.1.other_ref, f32[8,128]{1,0:T(8,128)S(1)} %get-tuple-element.60.info_ref, ...), custom_call_target="tpu_custom_call" | custom-call | tf_op jit(solution)/shard_map/cond/branch_1_fun/factor_rows/pallas_call | solution.py:686
  73.0 17.8 %all_to_all.20.sums_ref = f32[256,1,128]{2,1,0:T(1,128)S(1)} all-to-all(f32[256,1,128]{2,1,0:T(1,128)S(1)} %bitcast.7), channel_id=1, replica_groups=mesh['z'=8,'x'=4,'y'=4,'c'=2] {'z','x','y','c'}, dimensions={0} | all-to-all | bytes 262144 | tf_op jit(solution)/shard_map/all_to_all | solution.py:744
  90.8 0.8 last.1
Async XLA Ops:
  3.3 20.3 %all-to-all-start.2 = ((f32[16,24,128]{2,1,0:T(8,128)}), f32[16,24,128]{2,1,0:T(8,128)S(1)}, u32[]{:S(2)}, u32[]{:S(2)}) async-start(f32[16,24,128]{2,1,0:T(8,128)} %prep.1), calls=%async_computation.2 | async-start | bytes 393216 | tf_op jit(solution)/shard_map/all_to_all | solution.py:726
  41.4 5.9 %collective-permute-start.1 = (f32[16,64,128]{2,1,0:T(8,128)S(1)}, f32[16,64,128]{2,1,0:T(8,128)S(1)}, u32[]{:S(2)}, u32[]{:S(2)}) collective-permute-start(f32[16,64,128]{2,1,0:T(8,128)S(1)} %all_to_all.19.mine_ref), channel_id=1, source_target_pairs={{0,1},{1,0},{2,3},{3,2},{4,5},{5,4},{6,7},{7,6},{8,9},{9,8},{10,11... | collective-permute-start | bytes 1572872 | tf_op jit(solution)/shard_map/cond/branch_1_fun/ppermute | solution.py:733
